TPU v7x, 32 devices: a whole 2x2x4 slice. The times are simulated.
32 devices in a mesh: dp: 4 (over x, core), sp: 8 (over z, y).
Axes of the slice: x: 2, y: 2, z: 4, core: 2. Of those that a mesh axis runs over, the one named last changes fastest.
Arguments:
- frames_in: bfloat16 [2048, 64, 256], P(('dp', 'sp')), may hold values from -6 to 6
- spatial_weight: bfloat16 [3, 3, 256, 256], replicated, may hold values from -0.125 to 0.125
- temporal_weight: bfloat16 [3, 256, 256], replicated, may hold values from -0.21875 to 0.21875
- cotangent: bfloat16 [2048, 64, 256], P(('dp', 'sp')), may hold values from -6 to 6
Outputs:
- block_out: bfloat16 [2048, 64, 256], P(('dp', 'sp'))
- grad_input: bfloat16 [2048, 64, 256], P(('dp', 'sp'))
- grad_spatial: float32 [3, 3, 256, 256], replicated
- grad_temporal: float32 [3, 256, 256], replicated
All inputs are finite; a program needn't handle non-finite values.
Results may differ from a plain program's by a relative error of at most 0.0049.
Values may be sent and summed in bfloat16 or wider, within the bound.
A program may use at most 128 MiB of HBM per device.

v0:
```python
import functools
import math

import jax
import jax.numpy as jnp
from jax import lax
from jax.experimental import pallas as pl
from jax.experimental.pallas import tpu as pltpu
from jax.sharding import PartitionSpec as P

FRAMES = 4
BLOCKS = 4
VMEM_LIMIT = 50 * 1024 * 1024
MESH = pl.DeviceIdType.MESH
F32 = jnp.float32
BF16 = jnp.bfloat16


def store_shifted(dest, offset, values, width):
    cells, channels = values.shape
    column = lax.broadcasted_iota(jnp.int32, (cells, channels), 0) % width
    before = jnp.where(column == 0, 0.0, pltpu.roll(values, 1, axis=0))
    after = jnp.where(column == width - 1, 0.0, pltpu.roll(values, cells - 1, axis=0))
    dest[pl.ds(offset, cells), 0:channels] = before.astype(BF16)
    dest[pl.ds(offset, cells), channels : 2 * channels] = values.astype(BF16)
    dest[pl.ds(offset, cells), 2 * channels : 3 * channels] = after.astype(BF16)


def zero_edges(dest, width):
    rows, lanes = dest.shape
    dest[0:width] = jnp.zeros((width, lanes), BF16)
    dest[rows - width : rows] = jnp.zeros((width, lanes), BF16)


def forward_kernel(width, x_ref, w_ref, act_ref, slope_ref, x3):
    step = pl.program_id(0)
    cells, channels = act_ref.shape

    @pl.when(step == 0)
    def _():
        zero_edges(x3, width)
        for block in range(BLOCKS):
            store_shifted(
                x3,
                width + block * cells,
                x_ref[block * cells : (block + 1) * cells].astype(F32),
                width,
            )

    base = pl.multiple_of(step * cells, cells)
    pre = jnp.zeros((cells, channels), F32)
    for tap in range(3):
        pre = pre + jnp.dot(
            x3[pl.ds(base + tap * width, cells), :], w_ref[tap], preferred_element_type=F32
        )
    sigma = jax.nn.sigmoid(pre)
    act_ref[...] = (pre * sigma).astype(BF16)
    slope_ref[...] = sigma * (1.0 + pre * (1.0 - sigma))


def backward_kernel(
    width, x_ref, cot_ref, cot1_ref, cot2_ref, act_ref, slope_ref, wt_ref, wf_ref,
    grad_in_ref, grads_ref, g3, temporal, spatial,
):
    step = pl.program_id(0)
    cells, channels = act_ref.shape

    @pl.when(step == 0)
    def _():
        zero_edges(g3, width)
        temporal[...] = jnp.zeros_like(temporal)
        spatial[...] = jnp.zeros_like(spatial)

    @pl.when(step < BLOCKS)
    def _():
        act_t = act_ref[...].T
        grad_act = jnp.zeros((cells, channels), F32)
        for tap, ref in enumerate((cot_ref, cot1_ref, cot2_ref)):
            grad_act = grad_act + jnp.dot(ref[...], wt_ref[tap], preferred_element_type=F32)
            temporal[tap] += jnp.dot(act_t, ref[...], preferred_element_type=F32)
        grad_pre = grad_act * slope_ref[...]
        store_shifted(g3, pl.multiple_of(width + step * cells, width), grad_pre, width)

    @pl.when(step >= BLOCKS)
    def _():
        base = pl.multiple_of((step - BLOCKS) * cells, cells)
        x_t = x_ref[...].T
        grad_in = cot_ref[...].astype(F32)
        for tap in range(3):
            window = g3[pl.ds(base + tap * width, cells), :]
            grad_in = grad_in + jnp.dot(window, wf_ref[tap], preferred_element_type=F32)
            spatial[tap] += jnp.dot(x_t, window, preferred_element_type=F32)
        grad_in_ref[...] = grad_in.astype(BF16)

    @pl.when(step == 2 * BLOCKS - 1)
    def _():
        for tap_row in range(3):
            for tap_col in range(3):
                place = (2 - tap_row) * 3 + 2 - tap_col
                grads_ref[place * channels : (place + 1) * channels] = spatial[
                    tap_row, :, tap_col * channels : (tap_col + 1) * channels
                ]
        for tap in range(3):
            grads_ref[(9 + tap) * channels : (10 + tap) * channels] = temporal[tap]


def temporal_kernel(x_ref, act_ref, act1_ref, act2_ref, w_ref, out_ref):
    total = jnp.dot(act_ref[...], w_ref[0], preferred_element_type=F32)
    total = total + jnp.dot(act1_ref[...], w_ref[1], preferred_element_type=F32)
    total = total + jnp.dot(act2_ref[...], w_ref[2], preferred_element_type=F32)
    total = total.astype(BF16).astype(F32)
    out_ref[...] = (x_ref[...].astype(F32) + total).astype(BF16)


def reduce_kernel(bits, chunks, grads_ref, full_ref, total, *scratch):
    levels = len(bits)
    staged = scratch[:chunks]
    recvs = scratch[chunks : chunks + chunks * levels]
    send_sem, recv_sem, back_send, back_recv = scratch[chunks + chunks * levels :]
    here = {name: lax.axis_index(name) for name in ("dp", "sp")}

    def partner(name, bit):
        mine = (here[name] // (1 << bit)) % 2
        ids = dict(here)
        ids[name] = here[name] + (1 - 2 * mine) * (1 << bit)
        return mine, (ids["dp"], ids["sp"])

    partners = [partner(name, bit) for name, bit in bits]
    barrier = pltpu.get_barrier_semaphore()
    for _, device in partners:
        pl.semaphore_signal(barrier, inc=1, device_id=device, device_id_type=MESH)
    pl.semaphore_wait(barrier, levels)

    rows = grads_ref.shape[0] // chunks
    half = grads_ref.shape[1] // 2
    rest = partners[1:]
    orders = []
    for chunk in range(chunks):
        turn = chunk % len(rest)
        orders.append(partners[:1] + rest[turn:] + rest[:turn])

    def send(chunk, level, source, dest, send_sems, recv_sems):
        copy = pltpu.make_async_remote_copy(
            src_ref=source,
            dst_ref=dest,
            send_sem=send_sems.at[chunk * levels + level],
            recv_sem=recv_sems.at[chunk * levels + level],
            device_id=orders[chunk][level][1],
            device_id_type=MESH,
        )
        copy.start()
        return copy

    mine = partners[0][0]
    keep = pl.multiple_of(mine * half, half)
    give = pl.multiple_of((1 - mine) * half, half)
    copies = [
        send(
            chunk, 0, grads_ref.at[chunk * rows : (chunk + 1) * rows, pl.ds(give, half)],
            recvs[chunk * levels], send_sem, recv_sem,
        )
        for chunk in range(chunks)
    ]
    for chunk in range(chunks):
        copies[chunk].wait()
        place = pl.ds(chunk * rows, rows)
        total[place, :] = grads_ref[place, pl.ds(keep, half)] + recvs[chunk * levels][...]
    starts = [[chunk * rows] for chunk in range(chunks)]
    size = rows
    for level in range(1, levels):
        size = size // 2
        copies = []
        for chunk in range(chunks):
            mine = orders[chunk][level][0]
            start = starts[chunk][-1]
            own = pl.multiple_of(start + mine * size, 16)
            other = pl.multiple_of(start + (1 - mine) * size, 16)
            source = total.at[pl.ds(other, size), :]
            if level == 1:
                staged[chunk][...] = total[pl.ds(other, size), :].astype(BF16)
                source = staged[chunk]
            dest = recvs[chunk * levels + level]
            copies.append(send(chunk, level, source, dest, send_sem, recv_sem))
            starts[chunk].append(own)
        for chunk in range(chunks):
            copies[chunk].wait()
            arrived = recvs[chunk * levels + level][...].astype(F32)
            total[pl.ds(starts[chunk][-1], size), :] += arrived
    for chunk in range(chunks):
        place = pl.ds(starts[chunk][-1], size)
        full_ref[place, pl.ds(keep, half)] = total[place, :].astype(BF16)
    for level in range(levels - 1, -1, -1):
        copies = []
        for chunk in range(chunks):
            place = full_ref.at[pl.ds(starts[chunk][level], size), pl.ds(keep, half)]
            copies.append(send(chunk, level, place, place, back_send, back_recv))
        for copy in copies:
            copy.wait()
        size = size * 2


def reduce_all(grads):
    bits = []
    for name in ("dp", "sp"):
        count = lax.axis_size(name)
        bits += [(name, bit) for bit in range(count.bit_length() - 1)]
    total_rows, channels = grads.shape
    half = channels // 2
    chunks = 3
    rows = total_rows // chunks
    levels = len(bits)
    staged = [pltpu.VMEM((rows // 2, half), BF16)] * chunks
    recvs = [
        pltpu.VMEM((rows >> level, half), BF16 if level == 1 else F32)
        for _ in range(chunks)
        for level in range(levels)
    ]
    semaphores = [pltpu.SemaphoreType.DMA((chunks * levels,))] * 4
    return pl.pallas_call(
        functools.partial(reduce_kernel, bits, chunks),
        out_shape=jax.ShapeDtypeStruct(grads.shape, BF16),
        in_specs=[pl.BlockSpec(memory_space=pltpu.VMEM)],
        out_specs=pl.BlockSpec(memory_space=pltpu.VMEM),
        scratch_shapes=[pltpu.VMEM((total_rows, half), F32)] + staged + recvs + semaphores,
        compiler_params=pltpu.CompilerParams(
            collective_id=0, has_side_effects=True, vmem_limit_bytes=VMEM_LIMIT
        ),
        name="reduce_all",
    )(grads)


def whole(array):
    return pl.BlockSpec(array.shape, lambda step: (0,) * array.ndim)


def local(frames_in, spatial_weight, temporal_weight, cotangent):
    slab_rows, width, channels = frames_in.shape
    sp_count = lax.axis_size("sp")
    cells = slab_rows * width
    block = cells // BLOCKS
    x = frames_in.reshape(cells, channels)
    cot = cotangent.reshape(cells, channels)
    params = pltpu.CompilerParams(
        dimension_semantics=("arbitrary",), vmem_limit_bytes=VMEM_LIMIT
    )

    def shift(values, by):
        pairs = [
            (i, i + by)
            for i in range(sp_count)
            if 0 <= i + by < sp_count and (i + by) // FRAMES == i // FRAMES
        ]
        return lax.ppermute(values, "sp", pairs)

    cot1 = shift(cot, -1)
    cot2 = shift(cot, -2)

    w3 = spatial_weight.reshape(3, 3 * channels, channels)
    wf = spatial_weight[::-1, ::-1].transpose(0, 1, 3, 2).reshape(3, 3 * channels, channels)
    wt = temporal_weight.transpose(0, 2, 1)
    rows_spec = pl.BlockSpec((block, channels), lambda step: (step, 0))
    frame = jax.ShapeDtypeStruct((cells, channels), BF16)
    padded = pltpu.VMEM((cells + 2 * width, 3 * channels), BF16)

    act, slope = pl.pallas_call(
        functools.partial(forward_kernel, width),
        grid=(BLOCKS,),
        out_shape=(frame, jax.ShapeDtypeStruct((cells, channels), F32)),
        in_specs=[whole(x), whole(w3)],
        out_specs=(rows_spec, rows_spec),
        scratch_shapes=[padded],
        compiler_params=params,
        cost_estimate=pl.CostEstimate(
            flops=18 * cells * channels * channels,
            bytes_accessed=8 * cells * channels,
            transcendentals=2 * cells * channels,
        ),
        name="forward",
    )(x, w3)

    act1 = shift(act, 1)
    act2 = shift(act, 2)

    first = pl.BlockSpec((block, channels), lambda step: (jnp.minimum(step, BLOCKS - 1), 0))
    second = pl.BlockSpec((block, channels), lambda step: (jnp.maximum(step - BLOCKS, 0), 0))
    both = pl.BlockSpec((block, channels), lambda step: (step % BLOCKS, 0))
    grads_shape = jax.ShapeDtypeStruct((12 * channels, channels), F32)
    grad_in, grads = pl.pallas_call(
        functools.partial(backward_kernel, width),
        grid=(2 * BLOCKS,),
        out_shape=(frame, grads_shape),
        in_specs=[second, both, first, first, first, first, whole(wt), whole(wf)],
        out_specs=(second, whole(grads_shape)),
        scratch_shapes=[
            padded,
            pltpu.VMEM((3, channels, channels), F32),
            pltpu.VMEM((3, channels, 3 * channels), F32),
        ],
        compiler_params=params,
        cost_estimate=pl.CostEstimate(
            flops=48 * cells * channels * channels,
            bytes_accessed=18 * cells * channels,
            transcendentals=0,
        ),
        name="backward",
    )(x, cot, cot1, cot2, act, slope, wt, wf)

    reduced = reduce_all(grads)

    block_out = pl.pallas_call(
        temporal_kernel,
        grid=(BLOCKS,),
        out_shape=frame,
        in_specs=[rows_spec] * 4 + [whole(temporal_weight)],
        out_specs=rows_spec,
        compiler_params=params,
        cost_estimate=pl.CostEstimate(
            flops=6 * cells * channels * channels,
            bytes_accessed=10 * cells * channels,
            transcendentals=0,
        ),
        name="temporal",
    )(x, act, act1, act2, temporal_weight)

    grad_scale = 1.0 / math.sqrt(slab_rows * sp_count * lax.axis_size("dp") * width)
    scaled = reduced.astype(F32) * grad_scale
    grad_spatial = scaled[: 9 * channels].reshape(3, 3, channels, channels)
    grad_temporal = scaled[9 * channels :].reshape(3, channels, channels)
    return (
        block_out.reshape(frames_in.shape),
        grad_in.reshape(frames_in.shape),
        grad_spatial,
        grad_temporal,
    )


def solution(mesh):
    placed = (P(("dp", "sp"), None, None), P(), P(), P(("dp", "sp"), None, None))
    return jax.shard_map(
        local,
        mesh=mesh,
        in_specs=placed,
        out_specs=(P(("dp", "sp"), None, None), P(("dp", "sp"), None, None), P(), P()),
        check_vma=False,
    )
```

profile of v0, /device:TPU:0, one launch (start us, length us, event | category | flops | bytes accessed | tf_op | source)
XLA Modules:
  0.0 174.5 jit_solution(9916546874861256089)
XLA Ops:
  0.6 1.3 collective-permute-start.3
  1.9 1.3 collective-permute-start.2
  3.2 0.0 copy-start.2
  3.2 1.3 copy-done.2
  4.5 0.0 copy-start.1
  4.5 9.7 %forward.1 = (bf16[4096,256]{1,0:T(8,128)(2,1)}, f32[4096,256]{1,0:T(8,128)}) custom-call(bf16[4096,256]{1,0:T(8,128)(2,1)} %bitcast.11, bf16[3,768,256]{2,1,0:T(8,128)(2,1)S(1)} %bitcast.14), custom_call_target="tpu_custom_call" | custom-call | flops 4831838208 | bytes 8388608 | tf_op jit(solution)/shard_map/forward/pallas_call | solution.py:265
  14.2 8.4 %collective-permute-start.1 = (bf16[4096,256]{1,0:T(8,128)(2,1)}, bf16[4096,256]{1,0:T(8,128)(2,1)}, u32[]{:S(2)}, u32[]{:S(2)}) collective-permute-start(bf16[4096,256]{1,0:T(8,128)(2,1)} %get-tuple-element.8.act_ref), channel_id=1, source_target_pairs={{0,2},{1,3},{4,6},{5,7},{8,10},{9,11},{12,14},{13,15},{16,18},{17,... | collective-permute-start | bytes 6291464 | tf_op jit(solution)/shard_map/ppermute | solution.py:253
  22.5 6.4 %collective-permute-start = (bf16[4096,256]{1,0:T(8,128)(2,1)}, bf16[4096,256]{1,0:T(8,128)(2,1)}, u32[]{:S(2)}, u32[]{:S(2)}) collective-permute-start(bf16[4096,256]{1,0:T(8,128)(2,1)} %get-tuple-element.8.act_ref), channel_id=1, source_target_pairs={{0,1},{1,2},{2,3},{4,5},{5,6},{6,7},{8,9},{9,10},{10,11},{12,13},{... | collective-permute-start | bytes 6291464 | tf_op jit(solution)/shard_map/ppermute | solution.py:253
  28.9 0.0 copy-done.1
  28.9 0.2 copy.8
  29.1 0.0 copy-start
  29.1 2.5 %reverse_bitcast_fusion = bf16[3,3,256,256]{2,3,1,0:T(8,128)(2,1)} fusion(bf16[3,3,256,256]{3,2,1,0:T(8,128)(2,1)} %param.5), kind=kLoop, calls=%fused_computation.1 | loop fusion | bytes 2359296 | tf_op jit(solution)/shard_map/transpose | solution.py:259
  31.6 2.4 %copy.9 = bf16[3,3,256,256]{3,2,1,0:T(8,128)(2,1)} copy(bf16[3,3,256,256]{2,3,1,0:T(8,128)(2,1)} %reverse_bitcast_fusion) | data formatting | bytes 2359296 | tf_op jit(solution)/shard_map/transpose | solution.py:259
  34.0 17.7 %collective-permute-done.3.cot2_ref = bf16[4096,256]{1,0:T(8,128)(2,1)} collective-permute-done((bf16[4096,256]{1,0:T(8,128)(2,1)}, bf16[4096,256]{1,0:T(8,128)(2,1)}, u32[]{:S(2)}, u32[]{:S(2)}) %collective-permute-start.3) | collective-permute-done | bytes 2097184 | tf_op jit(solution)/shard_map/ppermute | solution.py:253
  51.7 1.0 collective-permute-done.2.cot1_ref
  52.7 0.0 copy-done
  52.7 0.0 copy-start.3
  52.8 1.3 copy-done.3
  54.0 20.0 %backward.1 = (bf16[4096,256]{1,0:T(8,128)(2,1)}, f32[3072,256]{1,0:T(8,128)}) custom-call(bf16[4096,256]{1,0:T(8,128)(2,1)S(1)} %bitcast.12, bf16[4096,256]{1,0:T(8,128)(2,1)} %bitcast.22, bf16[4096,256]{1,0:T(8,128)(2,1)} %collective-permute-done.2.cot1_ref, bf16[4096,256]{1,0:T(8,128)(2,1)} %collective-permute-done.3.cot2_ref, ...), custom_call_target="tpu_custom_call" | custom-call | flops 12884901888 | bytes 18874368 | tf_op jit(solution)/shard_map/backward/pallas_call | solution.py:288
  74.0 92.0 %reduce_all.1 = bf16[3072,256]{1,0:T(8,128)(2,1)S(1)} custom-call(f32[3072,256]{1,0:T(8,128)} %get-tuple-element.11.grads_ref), custom_call_target="tpu_custom_call" | custom-call | tf_op jit(solution)/shard_map/reduce_all/pallas_call | solution.py:219
  166.0 0.3 convert_multiply_fusion
  166.3 0.9 slice.9
  167.3 1.6 slice.8
  168.8 0.0 collective-permute-done.1.act2_ref
  168.8 0.0 collective-permute-done.act1_ref
  168.8 5.7 %temporal.1 = bf16[4096,256]{1,0:T(8,128)(2,1)} custom-call(bf16[4096,256]{1,0:T(8,128)(2,1)S(1)} %bitcast.13, bf16[4096,256]{1,0:T(8,128)(2,1)} %get-tuple-element.8.act_ref, bf16[4096,256]{1,0:T(8,128)(2,1)} %collective-permute-done.act1_ref, bf16[4096,256]{1,0:T(8,128)(2,1)} %collective-permute-done.1.act2_ref, bf16[3,256,256]{2,1,0:T(8,128)(2,1)S(1)} %copy-done.1), custom_call_target="tpu_custom_call" | custom-call | flops 1610612736 | bytes 10485760 | tf_op jit(solution)/shard_map/temporal/pallas_call | solution.py:310
Async XLA Ops:
  0.6 51.1 %collective-permute-start.3 = (bf16[4096,256]{1,0:T(8,128)(2,1)}, bf16[4096,256]{1,0:T(8,128)(2,1)}, u32[]{:S(2)}, u32[]{:S(2)}) collective-permute-start(bf16[4096,256]{1,0:T(8,128)(2,1)} %bitcast.20), channel_id=1, source_target_pairs={{2,0},{3,1},{6,4},{7,5},{10,8},{11,9},{14,12},{15,13},{18,16},{19,... | collective-permute-start | bytes 6291464 | tf_op jit(solution)/shard_map/ppermute | solution.py:253
  1.9 50.8 %collective-permute-start.2 = (bf16[4096,256]{1,0:T(8,128)(2,1)}, bf16[4096,256]{1,0:T(8,128)(2,1)}, u32[]{:S(2)}, u32[]{:S(2)}) collective-permute-start(bf16[4096,256]{1,0:T(8,128)(2,1)} %bitcast.21), channel_id=1, source_target_pairs={{1,0},{2,1},{3,2},{5,4},{6,5},{7,6},{9,8},{10,9},{11,10},{13,12},{... | collective-permute-start | bytes 6291464 | tf_op jit(solution)/shard_map/ppermute | solution.py:253
  3.2 1.3 copy-start.2
  4.5 24.4 %copy-start.1 = (bf16[3,256,256]{2,1,0:T(8,128)(2,1)S(1)}, bf16[3,256,256]{2,1,0:T(8,128)(2,1)}, u32[]{:S(2)}) copy-start(bf16[3,256,256]{2,1,0:T(8,128)(2,1)} %w_ref.1) | copy-start | bytes 1179652
  14.2 154.7 %collective-permute-start.1 = (bf16[4096,256]{1,0:T(8,128)(2,1)}, bf16[4096,256]{1,0:T(8,128)(2,1)}, u32[]{:S(2)}, u32[]{:S(2)}) collective-permute-start(bf16[4096,256]{1,0:T(8,128)(2,1)} %get-tuple-element.8.act_ref), channel_id=1, source_target_pairs={{0,2},{1,3},{4,6},{5,7},{8,10},{9,11},{12,14},{13,15},{16,18},{17,... | collective-permute-start | bytes 6291464 | tf_op jit(solution)/shard_map/ppermute | solution.py:253
  22.5 146.3 %collective-permute-start = (bf16[4096,256]{1,0:T(8,128)(2,1)}, bf16[4096,256]{1,0:T(8,128)(2,1)}, u32[]{:S(2)}, u32[]{:S(2)}) collective-permute-start(bf16[4096,256]{1,0:T(8,128)(2,1)} %get-tuple-element.8.act_ref), channel_id=1, source_target_pairs={{0,1},{1,2},{2,3},{4,5},{5,6},{6,7},{8,9},{9,10},{10,11},{12,13},{... | collective-permute-start | bytes 6291464 | tf_op jit(solution)/shard_map/ppermute | solution.py:253
  29.1 23.6 %copy-start = (bf16[64,64,256]{2,1,0:T(8,128)(2,1)S(1)}, bf16[64,64,256]{2,1,0:T(8,128)(2,1)}, u32[]{:S(2)}) copy-start(bf16[64,64,256]{2,1,0:T(8,128)(2,1)} %param.4) | copy-start | bytes 6291460
  52.7 1.3 copy-start.3
where the time goes:
time: 175 us; the launch traced here: 174 us
  Pallas kernels  127 us (73%)
  waiting for transfers between devices  18.7 us (11%)
  starting transfers between devices  17.4 us (10%)
  local copies, waits for them, and re-layouts  10.1 us (6%)
    pallas_call x1, Pallas kernels, reduce_all(): pl.pallas_call(functools.partial(reduce_kernel, bits, chunks), out_shape=...  92 us
    pallas_call x1, Pallas kernels, local(): pl.pallas_call(functools.partial(backward_kernel, width), grid=(2 * BLOCK...  20 us
    ppermute x4, waiting for transfers between devices, shift(): return lax.ppermute(values, 'sp', pairs)  18.7 us
    ppermute x4, starting transfers between devices, shift(): return lax.ppermute(values, 'sp', pairs)  17.4 us
    pallas_call x1, Pallas kernels, local(): pl.pallas_call(functools.partial(forward_kernel, width), grid=(BLOCKS,),...  9.65 us
    pallas_call x1, Pallas kernels, local(): pl.pallas_call(temporal_kernel, grid=(BLOCKS,), out_shape=frame, in_specs...  5.65 us
    transpose x2, local copies, waits for them, and re-layouts, local(): spatial_weight[::-1, ::-1].transpose(0, 1, 3, 2)  4.88 us
  transfers between devices with their start and end apart: 4, of which 2 were waited for; matrix products, arithmetic and copies ran while one was open for 4% of the time, Pallas kernels for 70%

commit v1 on v0

v1 whole, which is shorter than its diff:
```python
import functools
import math

import jax
import jax.numpy as jnp
from jax import lax
from jax.experimental import pallas as pl
from jax.experimental.pallas import tpu as pltpu
from jax.sharding import PartitionSpec as P

FRAMES = 4
CHUNKS = 8
HALF = CHUNKS // 2
VMEM_LIMIT = 58 * 1024 * 1024
MESH = pl.DeviceIdType.MESH
F32 = jnp.float32
BF16 = jnp.bfloat16


def mm(left, right):
    return jnp.dot(left, right, preferred_element_type=F32)


def store_shifted(dest, offset, values, width):
    cells, channels = values.shape
    column = lax.broadcasted_iota(jnp.int32, (cells, channels), 0) % width
    before = jnp.where(column == 0, 0.0, pltpu.roll(values, 1, axis=0))
    after = jnp.where(column == width - 1, 0.0, pltpu.roll(values, cells - 1, axis=0))
    dest[pl.ds(offset, cells), 0:channels] = before.astype(BF16)
    dest[pl.ds(offset, cells), channels : 2 * channels] = values.astype(BF16)
    dest[pl.ds(offset, cells), 2 * channels : 3 * channels] = after.astype(BF16)


def zero_edges(dest, width):
    rows, lanes = dest.shape
    dest[0:width] = jnp.zeros((width, lanes), BF16)
    dest[rows - width : rows] = jnp.zeros((width, lanes), BF16)


def block_kernel(
    width, members, scale,
    x_hbm, cot_hbm, w_ref, tw_ref,
    out_ref, gin_ref, full,
    x, cot, c1, c2, a1, a2, act, slope, x3, g3, wf, wt, part, acc,
    core_in, total, stage, x_in1, x_in2, z_in1, z_in2, slots,
    load_sem, c1_sem, c2_sem, a1_sem, a2_sem, cy_sem, cz_sem, ay_sem, az_sem, rc_sem, ra_sem,
    red_send, red_recv,
):
    dp = lax.axis_index("dp")
    sp = lax.axis_index("sp")
    frame = sp % FRAMES
    y = sp % 2
    zi = (sp // 2) % 4
    group = sp // 8
    member = y + 2 * group
    core = dp % 2
    mx = (dp // 2) % 2
    cells, channels = out_ref.shape
    size = cells // CHUNKS
    lanes = channels // 2

    y_dev = (dp, sp + 1 - 2 * y)
    t_dev = (dp, sp + 2 - 4 * (zi % 2))
    core_dev = (dp + 1 - 2 * core, sp)
    x_dev = (dp + 2 - 4 * mx, sp)

    def z_member(offset):
        return (zi + offset) % 4

    def z_dev(offset):
        return (dp, sp + (z_member(offset) - zi) * 2)

    def m_dev(offset):
        other = (member + offset) % members
        return (dp, sp + other % 2 - y + (other // 2 - group) * 8)

    def chunk(ref, index):
        return ref.at[pl.ds(pl.multiple_of(index * size, size), size), :]

    def copy(source, dest, send_sem, recv_sem, device):
        return pltpu.make_async_remote_copy(
            src_ref=source, dst_ref=dest, send_sem=send_sem, recv_sem=recv_sem,
            device_id=device, device_id_type=MESH,
        )

    def send(source, dest, index, send_sems, recv_sems, device):
        copy(
            chunk(source, index), chunk(dest, index), send_sems.at[index], recv_sems.at[index], device
        ).start()

    def arrived(dest, index, recv_sems):
        copy(
            chunk(dest, index), chunk(dest, index), recv_sems.at[index], recv_sems.at[index], y_dev
        ).wait_recv()

    def left(index, send_sems):
        copy(
            chunk(act, index), chunk(act, index), send_sems.at[index], send_sems.at[index], y_dev
        ).wait_send()

    def each(start, stop, body):
        def step(index, carry):
            body(index)
            return carry

        lax.fori_loop(start, stop, step, 0)

    x_load = pltpu.make_async_copy(x_hbm, x, load_sem.at[0])
    cot_load = pltpu.make_async_copy(cot_hbm, cot, load_sem.at[1])
    x_load.start()
    cot_load.start()

    barrier = pltpu.get_barrier_semaphore()
    greeted = [core_dev, x_dev] + [z_dev(i) for i in (1, 2, 3)] + [m_dev(i) for i in range(1, members)]
    for device in greeted:
        pl.semaphore_signal(barrier, inc=1, device_id=device, device_id_type=MESH)
    pl.semaphore_wait(barrier, len(greeted))

    @pl.when(frame == 1)
    def _():
        each(0, CHUNKS, lambda i: send(cot_hbm, c1, i, cy_sem, c1_sem, y_dev))

    @pl.when(frame == 2)
    def _():
        each(0, CHUNKS, lambda i: send(cot_hbm, c2, i, cz_sem, c2_sem, t_dev))
        each(HALF, CHUNKS, lambda i: send(cot_hbm, c1, i, cy_sem, c1_sem, y_dev))

    @pl.when(frame == 3)
    def _():
        each(0, CHUNKS, lambda i: send(cot_hbm, c1, i, cy_sem, c1_sem, y_dev))
        each(0, HALF, lambda i: send(cot_hbm, c2, i, cz_sem, c2_sem, t_dev))

    acc[...] = jnp.zeros_like(acc)
    zero_edges(x3, width)
    zero_edges(g3, width)
    x_load.wait()

    def forward(step):
        @pl.when(step < CHUNKS)
        def _():
            store_shifted(
                x3, pl.multiple_of(width + step * size, width),
                x[pl.ds(pl.multiple_of(step * size, size), size), :].astype(F32), width,
            )

        @pl.when(step >= 1)
        def _():
            index = step - 1
            base = pl.multiple_of(index * size, size)
            pre = jnp.zeros((size, channels), F32)
            for tap in range(3):
                pre = pre + mm(x3[pl.ds(base + tap * width, size), :], w_ref[tap])
            sigma = jax.nn.sigmoid(pre)
            act[pl.ds(base, size), :] = (pre * sigma).astype(BF16)
            slope[pl.ds(base, size), :] = sigma * (1.0 + pre * (1.0 - sigma))

            @pl.when(frame == 0)
            def _():
                send(act, a2, index, az_sem, a2_sem, t_dev)

            @pl.when((frame == 0) & (index == 0))
            def _():
                send(act, a1, index, ay_sem, a1_sem, y_dev)

            @pl.when((frame == 1) & (index < HALF))
            def _():
                send(act, a1, index, ay_sem, a1_sem, y_dev)

            @pl.when((frame == 1) & (index >= HALF))
            def _():
                send(act, a2, index, az_sem, a2_sem, t_dev)

            @pl.when(frame == 2)
            def _():
                send(act, a1, index, ay_sem, a1_sem, y_dev)

    each(0, CHUNKS + 1, forward)

    @pl.when(frame == 1)
    def _():
        each(0, HALF, lambda i: send(act, a2, i, az_sem, a2_sem, t_dev))

    for tap in range(3):
        wt[tap] = tw_ref[tap].T
        for side in range(3):
            wf[tap, side * channels : (side + 1) * channels, :] = w_ref[
                2 - tap, (2 - side) * channels : (3 - side) * channels, :
            ].T
    cot_load.wait()

    gt_base = 9 * channels

    def add_temporal(tap, act_t, other):
        acc[gt_base + tap * channels : gt_base + (tap + 1) * channels, :] += mm(act_t, other)

    def backward(index):
        base = pl.multiple_of(index * size, size)
        rows = pl.ds(base, size)
        early = index < HALF

        @pl.when((frame < 3) | (index >= HALF))
        def _():
            arrived(c1, index, c1_sem)

        @pl.when((frame == 0) | ((frame == 1) & early))
        def _():
            arrived(c2, index, c2_sem)

        @pl.when((frame == 0) & early)
        def _():
            send(c2, c1, index, rc_sem, c1_sem, y_dev)

        @pl.when((frame == 0) & (index == HALF - 1))
        def _():
            each(1, CHUNKS, lambda i: send(act, a1, i, ay_sem, a1_sem, y_dev))

        @pl.when((frame == 3) & (index >= HALF))
        def _():
            c2[rows, :] = (mm(c1[rows, :], wt[1]) + mm(cot[rows, :], wt[2])).astype(BF16)
            send(c2, c1, index, cz_sem, c1_sem, t_dev)

        act_t = act[rows, :].T
        part[...] = mm(cot[rows, :], wt[0])
        add_temporal(0, act_t, cot[rows, :])

        @pl.when((frame == 0) | (frame == 2) | ((frame == 1) & early))
        def _():
            part[...] += mm(c1[rows, :], wt[1])
            add_temporal(1, act_t, c1[rows, :])

        @pl.when((frame == 0) | ((frame == 1) & early))
        def _():
            part[...] += mm(c2[rows, :], wt[2])
            add_temporal(2, act_t, c2[rows, :])

        @pl.when((frame == 1) & (index >= HALF))
        def _():
            part[...] += c1[rows, :].astype(F32)

        grad_pre = part[...].astype(BF16).astype(F32) * slope[rows, :]
        store_shifted(g3, pl.multiple_of(width + base, width), grad_pre, width)
        grad_pre = grad_pre.astype(BF16)
        for tap in range(3):
            window = x3[pl.ds(base + tap * width, size), :]
            acc[tap * 3 * channels : (tap + 1) * 3 * channels, :] += mm(window.T, grad_pre)

    each(0, CHUNKS, backward)

    @pl.when(frame == 3)
    def _():
        def late(index):
            rows = pl.ds(pl.multiple_of(index * size, size), size)
            arrived(a2, index, a2_sem)
            send(a2, a1, index, ra_sem, a1_sem, y_dev)
            act_t = a2[rows, :].T
            add_temporal(1, act_t, c1[rows, :])
            add_temporal(2, act_t, cot[rows, :])

        each(HALF, CHUNKS, late)

    def relay(index):
        @pl.when(frame == 0)
        def _():
            arrived(a1, index, a1_sem)
            send(a1, a1, index, ra_sem, a1_sem, t_dev)

    def grad_input(index):
        base = pl.multiple_of(index * size, size)
        total_in = cot[pl.ds(base, size), :].astype(F32)
        for tap in range(3):
            total_in = total_in + mm(g3[pl.ds(base + tap * width, size), :], wf[tap])
        gin_ref[pl.ds(base, size), :] = total_in.astype(BF16)

    def output(index):
        rows = pl.ds(pl.multiple_of(index * size, size), size)

        @pl.when(frame >= 1)
        def _():
            arrived(a1, index, a1_sem)

        @pl.when((frame == 2) | ((frame == 3) & (index < HALF)))
        def _():
            arrived(a2, index, a2_sem)

        part[...] = mm(act[rows, :], tw_ref[0])

        @pl.when(frame >= 1)
        def _():
            part[...] += mm(a1[rows, :], tw_ref[1])

        @pl.when(frame >= 2)
        def _():
            part[...] += mm(a2[rows, :], tw_ref[2])

        temporal = part[...].astype(BF16).astype(F32)
        out_ref[rows, :] = (x[rows, :].astype(F32) + temporal).astype(BF16)

    count = acc.shape[0]
    n1 = count // 3 * 2
    h1, q1 = n1 // 2, n1 // 8
    q2 = (count - n1) // 4
    e2 = q2 // 2
    keep = pl.multiple_of(core * lanes, lanes)
    give = pl.multiple_of((1 - core) * lanes, lanes)
    used = []

    def exchange(source, dest, device):
        slot = len(used)
        moved = copy(source, dest, red_send.at[slot], red_recv.at[slot], device)
        moved.start()
        used.append(moved)
        return moved

    def rows_of(start, length):
        return pl.ds(pl.multiple_of(start, 16), length)

    own_half, other_half = rows_of(mx * h1, h1), rows_of((1 - mx) * h1, h1)

    def piece1(offset):
        return rows_of(mx * h1 + z_member(offset) * q1, q1)

    def piece2(offset):
        return rows_of(n1 + z_member(offset) * q2, q2)

    def quarter2(which):
        return rows_of(n1 + zi * q2 + which * e2, e2)

    moves = [exchange(acc.at[:, pl.ds(give, lanes)], core_in, core_dev)]
    each(0, 2, grad_input)
    moves[0].wait()
    summed = acc[:, pl.ds(keep, lanes)] + core_in[...]
    total[...] = summed
    stage[...] = summed.astype(BF16)

    moves = [exchange(stage.at[other_half, :], x_in1, x_dev)]
    moves += [exchange(stage.at[piece2(i), :], z_in2.at[i - 1], z_dev(i)) for i in (2, 1, 3)]
    each(2, 5, grad_input)
    relay(0)
    for moved in moves:
        moved.wait()
    summed = total[own_half, :] + x_in1[...].astype(F32)
    total[own_half, :] = summed
    stage[own_half, :] = summed.astype(BF16)
    summed = total[piece2(0), :]
    for i in range(3):
        summed = summed + z_in2[i].astype(F32)
    total[piece2(0), :] = summed
    stage[piece2(0), :] = summed.astype(BF16)

    moves = [exchange(stage.at[piece1(i), :], z_in1.at[i - 1], z_dev(i)) for i in (2, 1, 3)]
    moves += [exchange(stage.at[quarter2(1 - mx), :], x_in2, x_dev)]
    each(5, CHUNKS, grad_input)
    relay(1)
    for moved in moves:
        moved.wait()
    summed = total[piece1(0), :]
    for i in range(3):
        summed = summed + z_in1[i].astype(F32)
    slots[member, 0:q1, :] = summed.astype(BF16)
    slots[member, q1 : q1 + e2, :] = (total[quarter2(mx), :] + x_in2[...].astype(F32)).astype(BF16)

    moves = [exchange(slots.at[member], slots.at[member], m_dev(i)) for i in range(1, members)]
    relay(2)
    for moved in moves:
        moved.wait()
    summed = slots[0].astype(F32)
    for i in range(1, members):
        summed = summed + slots[i].astype(F32)
    summed = (summed * scale).astype(BF16)
    mine = pl.ds(keep, lanes)
    full[piece1(0), mine] = summed[0:q1]
    full[quarter2(mx), mine] = summed[q1 : q1 + e2]

    def spread(rows, device):
        place = full.at[rows, mine]
        return exchange(place, place, device)

    moves = [spread(piece1(0), z_dev(i)) for i in (2, 1, 3)] + [spread(quarter2(mx), x_dev)]
    relay(3)
    each(HALF, CHUNKS, output)
    for moved in moves:
        moved.wait()
    moves = [spread(own_half, x_dev)] + [spread(piece2(0), z_dev(i)) for i in (2, 1, 3)]
    shared = [spread(own_half, core_dev), spread(piece2(0), core_dev)]
    each(0, HALF, output)
    for moved in moves:
        moved.wait()
    shared += [spread(other_half, core_dev)] + [spread(piece2(i), core_dev) for i in (1, 2, 3)]
    for moved in shared:
        moved.wait()

    @pl.when(frame == 0)
    def _():
        each(0, HALF, lambda i: left(i, rc_sem))
        each(0, HALF, lambda i: left(i, ra_sem))
        each(0, CHUNKS, lambda i: left(i, ay_sem))
        each(0, CHUNKS, lambda i: left(i, az_sem))

    @pl.when(frame == 1)
    def _():
        each(0, CHUNKS, lambda i: left(i, cy_sem))
        each(0, HALF, lambda i: left(i, ay_sem))
        each(0, CHUNKS, lambda i: left(i, az_sem))

    @pl.when(frame == 2)
    def _():
        each(0, CHUNKS, lambda i: left(i, cz_sem))
        each(HALF, CHUNKS, lambda i: left(i, cy_sem))
        each(0, CHUNKS, lambda i: left(i, ay_sem))

    @pl.when(frame == 3)
    def _():
        each(0, CHUNKS, lambda i: left(i, cy_sem))
        each(0, CHUNKS, lambda i: left(i, cz_sem))
        each(HALF, CHUNKS, lambda i: left(i, ra_sem))


def local(frames_in, spatial_weight, temporal_weight, cotangent):
    slab_rows, width, channels = frames_in.shape
    sp_count = lax.axis_size("sp")
    dp_count = lax.axis_size("dp")
    members = sp_count // 4
    cells = slab_rows * width
    size = cells // CHUNKS
    lanes = channels // 2
    x = frames_in.reshape(cells, channels)
    cot = cotangent.reshape(cells, channels)
    w3 = spatial_weight.reshape(3, 3 * channels, channels)
    scale = 1.0 / math.sqrt(slab_rows * sp_count * dp_count * width)

    count = 12 * channels
    h1, q1 = count // 3, count // 12
    q2 = count // 12
    e2 = q2 // 2
    exchanges = 23 + members - 1
    frame = jax.ShapeDtypeStruct((cells, channels), BF16)
    slab = pltpu.VMEM((cells, channels), BF16)
    padded = pltpu.VMEM((cells + 2 * width, 3 * channels), BF16)
    vmem = pl.BlockSpec(memory_space=pltpu.VMEM)
    hbm = pl.BlockSpec(memory_space=pl.ANY)
    block_out, grad_in, grads = pl.pallas_call(
        functools.partial(block_kernel, width, members, scale),
        out_shape=(frame, frame, jax.ShapeDtypeStruct((count, channels), BF16)),
        in_specs=[hbm, hbm, vmem, vmem],
        out_specs=(vmem, vmem, vmem),
        scratch_shapes=[slab] * 7
        + [
            pltpu.VMEM((cells, channels), F32),
            padded,
            padded,
            pltpu.VMEM((3, 3 * channels, channels), BF16),
            pltpu.VMEM((3, channels, channels), BF16),
            pltpu.VMEM((size, channels), F32),
            pltpu.VMEM((count, channels), F32),
            pltpu.VMEM((count, lanes), F32),
            pltpu.VMEM((count, lanes), F32),
            pltpu.VMEM((count, lanes), BF16),
            pltpu.VMEM((h1, lanes), BF16),
            pltpu.VMEM((e2, lanes), BF16),
            pltpu.VMEM((3, q1, lanes), BF16),
            pltpu.VMEM((3, q2, lanes), BF16),
            pltpu.VMEM((members, q1 + e2, lanes), BF16),
            pltpu.SemaphoreType.DMA((2,)),
        ]
        + [pltpu.SemaphoreType.DMA((CHUNKS,))] * 10
        + [pltpu.SemaphoreType.DMA((exchanges,))] * 2,
        compiler_params=pltpu.CompilerParams(
            collective_id=0, has_side_effects=True, vmem_limit_bytes=VMEM_LIMIT
        ),
        cost_estimate=pl.CostEstimate(
            flops=72 * cells * channels * channels,
            bytes_accessed=16 * cells * channels,
            transcendentals=2 * cells * channels,
        ),
        name="video_block",
    )(x, cot, w3, temporal_weight)

    grads = grads.astype(F32)
    grad_spatial = grads[: 9 * channels].reshape(3, 3, channels, channels)
    grad_temporal = grads[9 * channels :].reshape(3, channels, channels)
    return (
        block_out.reshape(frames_in.shape),
        grad_in.reshape(frames_in.shape),
        grad_spatial,
        grad_temporal,
    )


def solution(mesh):
    placed = (P(("dp", "sp"), None, None), P(), P(), P(("dp", "sp"), None, None))
    return jax.shard_map(
        local,
        mesh=mesh,
        in_specs=placed,
        out_specs=(P(("dp", "sp"), None, None), P(("dp", "sp"), None, None), P(), P()),
        check_vma=False,
    )
```

time: 175 us -> 114 us (0.65)
  Pallas kernels: 127 us -> 105 us
  waiting for transfers between devices: 18.7 us -> 0 us
  starting transfers between devices: 17.4 us -> 0 us
  local copies, waits for them, and re-layouts: 10.1 us -> 8.16 us
    pallas_call x4 -> x1, Pallas kernels: 127 us -> 105 us  [local(): pl.pallas_call(functools.partial(block_kernel, width, members, scale), ou...]
    ppermute x4 -> x0, waiting for transfers between devices: 18.7 us -> none  [shift(): return lax.ppermute(values, 'sp', pairs)]
    ppermute x4 -> x0, starting transfers between devices: 17.4 us -> none  [shift(): return lax.ppermute(values, 'sp', pairs)]
    transpose x2 -> x0, local copies, waits for them, and re-layouts: 4.88 us -> none  [local(): spatial_weight[::-1, ::-1].transpose(0, 1, 3, 2)]
    unnamed x9 -> x8, local copies, waits for them, and re-layouts: 2.72 us -> 4.53 us
  transfers between devices with their start and end apart: 4 -> 0, of which waited for: 2 -> 0; matrix products, arithmetic and copies ran while one was open for 4% -> 0% of each run, Pallas kernels for 70% -> 0%
where the time goes in v1:
time: 114 us
  Pallas kernels  105 us (92%)
  local copies, waits for them, and re-layouts  8.16 us (7%)
    pallas_call x1, Pallas kernels, local(): pl.pallas_call(functools.partial(block_kernel, width, members, scale), ou...  105 us
    unnamed x8, local copies, waits for them, and re-layouts  4.53 us

profile of v1, /device:TPU:0, one launch (start us, length us, event | category | flops | bytes accessed | tf_op | source)
XLA Modules:
  0.0 113.9 jit_solution(14323782206619415472)
XLA Ops:
  0.6 105.1 %video_block.1 = (bf16[4096,256]{1,0:T(8,128)(2,1)}, bf16[4096,256]{1,0:T(8,128)(2,1)}, bf16[3072,256]{1,0:T(8,128)(2,1)}) custom-call(bf16[4096,256]{1,0:T(8,128)(2,1)} %bitcast.11, bf16[4096,256]{1,0:T(8,128)(2,1)} %bitcast.12, bf16[3,768,256]{2,1,0:T(8,128)(2,1)} %bitcast.13, bf16[3,256,256]{2,1,0:T(8,128)(2,1)} %tw_ref.1), custom_call_target="tpu_custom_call" | custom-call | flops 19327352832 | bytes 16777216 | tf_op jit(solution)/shard_map/video_block/pallas_call | solution.py:441
  105.8 0.0 copy-start
  105.8 2.0 %slice.9 = f32[768,256]{1,0:T(8,128)} slice(bf16[3072,256]{1,0:T(8,128)(2,1)} %get-tuple-element.9), slice={[2304:3072], [0:256]} | slice | bytes 1572864 | tf_op jit(solution)/shard_map/slice | solution.py:480
  107.8 0.0 copy-done
  107.8 0.0 copy-start.2
  107.8 1.6 %slice.8 = f32[2304,256]{1,0:T(8,128)} slice(bf16[3072,256]{1,0:T(8,128)(2,1)S(1)} %copy-done), slice={[0:2304], [0:256]} | slice | bytes 4718592 | tf_op jit(solution)/shard_map/slice | solution.py:479
  109.4 0.9 copy-done.2
  110.3 0.0 copy-start.1
  110.3 1.3 %copy.10 = bf16[64,64,256]{2,1,0:T(8,128)(2,1)} copy(bf16[64,64,256]{2,1,0:T(8,128)(2,1)S(1)} %bitcast.9) | data formatting | bytes 4194304
  111.6 1.0 copy-done.1
  112.6 1.3 %copy.11 = bf16[64,64,256]{2,1,0:T(8,128)(2,1)} copy(bf16[64,64,256]{2,1,0:T(8,128)(2,1)S(1)} %bitcast.8) | data formatting | bytes 4194304
Async XLA Ops:
  105.8 2.1 %copy-start = (bf16[3072,256]{1,0:T(8,128)(2,1)S(1)}, bf16[3072,256]{1,0:T(8,128)(2,1)}, u32[]{:S(2)}) copy-start(bf16[3072,256]{1,0:T(8,128)(2,1)} %get-tuple-element.9) | copy-start | bytes 4718596
  107.8 2.4 %copy-start.2 = (bf16[4096,256]{1,0:T(8,128)(2,1)S(1)}, bf16[4096,256]{1,0:T(8,128)(2,1)}, u32[]{:S(2)}) copy-start(bf16[4096,256]{1,0:T(8,128)(2,1)} %get-tuple-element.7) | copy-start | bytes 6291460
  110.3 2.3 %copy-start.1 = (bf16[4096,256]{1,0:T(8,128)(2,1)S(1)}, bf16[4096,256]{1,0:T(8,128)(2,1)}, u32[]{:S(2)}) copy-start(bf16[4096,256]{1,0:T(8,128)(2,1)} %get-tuple-element.8) | copy-start | bytes 6291460

commit v2 on v1

--- a/solution.py
+++ b/solution.py
@@ -11,6 +11,14 @@
 FRAMES = 4
 CHUNKS = 8
 HALF = CHUNKS // 2
+LEAD = CHUNKS // 8
+VIA = 2
+HOLD = 1
+HELD_AT = (19.3,)
+GRAD_INPUT_AT = ((1, 3.0), (0, 3.1))
+RELAY_AT = (2.5, 13.5)
+LAST_AT = (19.5, 19.6)
+OUTPUT_AT = ((20.5, 4, 5), (20.6, 5, 6), (22.5, 6, 7), (28.0, 0, 2), (28.1, 7, 8), (28.2, 3, 4), (28.3, 2, 3))
 VMEM_LIMIT = 58 * 1024 * 1024
 MESH = pl.DeviceIdType.MESH
 F32 = jnp.float32
@@ -40,11 +48,11 @@
 def block_kernel(
     width, members, scale,
     x_hbm, cot_hbm, w_ref, tw_ref,
-    out_ref, gin_ref, full,
-    x, cot, c1, c2, a1, a2, act, slope, x3, g3, wf, wt, part, acc,
-    core_in, total, stage, x_in1, x_in2, z_in1, z_in2, slots,
+    out_hbm, gin_hbm, full,
+    x, cot, c1, c2, a1, a2, act, out, gin, slope, x3, g3, wf, wt, part, acc,
+    core_in, total, stage, x_in, z_in, slots,
     load_sem, c1_sem, c2_sem, a1_sem, a2_sem, cy_sem, cz_sem, ay_sem, az_sem, rc_sem, ra_sem,
-    red_send, red_recv,
+    out_sem, gin_sem, red_send, red_recv,
 ):
     dp = lax.axis_index("dp")
     sp = lax.axis_index("sp")
@@ -55,7 +63,7 @@
     member = y + 2 * group
     core = dp % 2
     mx = (dp // 2) % 2
-    cells, channels = out_ref.shape
+    cells, channels = x.shape
     size = cells // CHUNKS
     lanes = channels // 2
 
@@ -158,11 +166,11 @@
             def _():
                 send(act, a2, index, az_sem, a2_sem, t_dev)
 
-            @pl.when((frame == 0) & (index == 0))
+            @pl.when((frame == 0) & (index < LEAD))
             def _():
                 send(act, a1, index, ay_sem, a1_sem, y_dev)
 
-            @pl.when((frame == 1) & (index < HALF))
+            @pl.when((frame == 1) & (index < VIA))
             def _():
                 send(act, a1, index, ay_sem, a1_sem, y_dev)
 
@@ -170,7 +178,7 @@
             def _():
                 send(act, a2, index, az_sem, a2_sem, t_dev)
 
-            @pl.when(frame == 2)
+            @pl.when((frame == 2) & (index < CHUNKS - HOLD))
             def _():
                 send(act, a1, index, ay_sem, a1_sem, y_dev)
 
@@ -178,7 +186,7 @@
 
     @pl.when(frame == 1)
     def _():
-        each(0, HALF, lambda i: send(act, a2, i, az_sem, a2_sem, t_dev))
+        each(0, HALF, lambda i: send(act, a2, HALF - 1 - i, az_sem, a2_sem, t_dev))
 
     for tap in range(3):
         wt[tap] = tw_ref[tap].T
@@ -189,36 +197,40 @@
     cot_load.wait()
 
     gt_base = 9 * channels
+    block = 3 * channels
 
     def add_temporal(tap, act_t, other):
         acc[gt_base + tap * channels : gt_base + (tap + 1) * channels, :] += mm(act_t, other)
 
-    def backward(index):
+    def receive(index):
+        rows = pl.ds(pl.multiple_of(index * size, size), size)
+        early = index < HALF
+
+        @pl.when((frame < 3) | (index >= HALF))
+        def _():
+            arrived(c1, index, c1_sem)
+
+        @pl.when((frame == 0) | ((frame == 1) & early))
+        def _():
+            arrived(c2, index, c2_sem)
+
+        @pl.when((frame == 0) & early)
+        def _():
+            send(c2, c1, index, rc_sem, c1_sem, y_dev)
+
+        @pl.when((frame == 0) & (index == HALF - 1))
+        def _():
+            each(LEAD, CHUNKS - HOLD, lambda i: send(act, a1, i, ay_sem, a1_sem, y_dev))
+
+        @pl.when((frame == 3) & (index >= HALF))
+        def _():
+            c2[rows, :] = (mm(c1[rows, :], wt[1]) + mm(cot[rows, :], wt[2])).astype(BF16)
+            send(c2, c1, index, cz_sem, c1_sem, t_dev)
+
+    def backward(index, finish):
         base = pl.multiple_of(index * size, size)
         rows = pl.ds(base, size)
         early = index < HALF
-
-        @pl.when((frame < 3) | (index >= HALF))
-        def _():
-            arrived(c1, index, c1_sem)
-
-        @pl.when((frame == 0) | ((frame == 1) & early))
-        def _():
-            arrived(c2, index, c2_sem)
-
-        @pl.when((frame == 0) & early)
-        def _():
-            send(c2, c1, index, rc_sem, c1_sem, y_dev)
-
-        @pl.when((frame == 0) & (index == HALF - 1))
-        def _():
-            each(1, CHUNKS, lambda i: send(act, a1, i, ay_sem, a1_sem, y_dev))
-
-        @pl.when((frame == 3) & (index >= HALF))
-        def _():
-            c2[rows, :] = (mm(c1[rows, :], wt[1]) + mm(cot[rows, :], wt[2])).astype(BF16)
-            send(c2, c1, index, cz_sem, c1_sem, t_dev)
-
         act_t = act[rows, :].T
         part[...] = mm(cot[rows, :], wt[0])
         add_temporal(0, act_t, cot[rows, :])
@@ -232,6 +244,8 @@
         def _():
             part[...] += mm(c2[rows, :], wt[2])
             add_temporal(2, act_t, c2[rows, :])
+
+        finish(0)
 
         @pl.when((frame == 1) & (index >= HALF))
         def _():
@@ -242,34 +256,16 @@
         grad_pre = grad_pre.astype(BF16)
         for tap in range(3):
             window = x3[pl.ds(base + tap * width, size), :]
-            acc[tap * 3 * channels : (tap + 1) * 3 * channels, :] += mm(window.T, grad_pre)
-
-    each(0, CHUNKS, backward)
-
-    @pl.when(frame == 3)
-    def _():
-        def late(index):
-            rows = pl.ds(pl.multiple_of(index * size, size), size)
-            arrived(a2, index, a2_sem)
-            send(a2, a1, index, ra_sem, a1_sem, y_dev)
-            act_t = a2[rows, :].T
-            add_temporal(1, act_t, c1[rows, :])
-            add_temporal(2, act_t, cot[rows, :])
-
-        each(HALF, CHUNKS, late)
-
-    def relay(index):
-        @pl.when(frame == 0)
-        def _():
-            arrived(a1, index, a1_sem)
-            send(a1, a1, index, ra_sem, a1_sem, t_dev)
+            acc[tap * block : (tap + 1) * block, :] += mm(window.T, grad_pre)
+            finish(1 + tap)
 
     def grad_input(index):
         base = pl.multiple_of(index * size, size)
         total_in = cot[pl.ds(base, size), :].astype(F32)
         for tap in range(3):
             total_in = total_in + mm(g3[pl.ds(base + tap * width, size), :], wf[tap])
-        gin_ref[pl.ds(base, size), :] = total_in.astype(BF16)
+        gin[pl.ds(base, size), :] = total_in.astype(BF16)
+        pltpu.make_async_copy(chunk(gin, index), chunk(gin_hbm, index), gin_sem.at[index]).start()
 
     def output(index):
         rows = pl.ds(pl.multiple_of(index * size, size), size)
@@ -278,7 +274,7 @@
         def _():
             arrived(a1, index, a1_sem)
 
-        @pl.when((frame == 2) | ((frame == 3) & (index < HALF)))
+        @pl.when((frame == 2) | ((frame == 3) & (index < VIA)))
         def _():
             arrived(a2, index, a2_sem)
 
@@ -293,113 +289,175 @@
             part[...] += mm(a2[rows, :], tw_ref[2])
 
         temporal = part[...].astype(BF16).astype(F32)
-        out_ref[rows, :] = (x[rows, :].astype(F32) + temporal).astype(BF16)
-
-    count = acc.shape[0]
-    n1 = count // 3 * 2
-    h1, q1 = n1 // 2, n1 // 8
-    q2 = (count - n1) // 4
-    e2 = q2 // 2
+        out[rows, :] = (x[rows, :].astype(F32) + temporal).astype(BF16)
+        pltpu.make_async_copy(chunk(out, index), chunk(out_hbm, index), out_sem.at[index]).start()
+
+    def relay_first(index):
+        @pl.when(frame == 0)
+        def _():
+            arrived(a1, index, a1_sem)
+            send(a1, a1, index, ra_sem, a1_sem, t_dev)
+
+    def relay_last(index):
+        @pl.when(frame == 3)
+        def _():
+            arrived(a2, index, a2_sem)
+            send(a2, a1, index, ra_sem, a1_sem, y_dev)
+
+    def held(index):
+        @pl.when((frame == 0) | (frame == 2))
+        def _():
+            send(act, a1, index, ay_sem, a1_sem, y_dev)
+
+    half, piece = block // 2, block // 8
     keep = pl.multiple_of(core * lanes, lanes)
     give = pl.multiple_of((1 - core) * lanes, lanes)
+    mine = pl.ds(keep, lanes)
+    bases = [gt_base] + [tap * block for tap in range(3)]
     used = []
-
-    def exchange(source, dest, device):
+    moving = {}
+
+    def exchange(name, source, dest, device):
         slot = len(used)
+        used.append(slot)
         moved = copy(source, dest, red_send.at[slot], red_recv.at[slot], device)
         moved.start()
-        used.append(moved)
-        return moved
+        moving.setdefault(name, []).append(moved)
+
+    def landed(name):
+        for moved in moving.pop(name):
+            moved.wait()
 
     def rows_of(start, length):
         return pl.ds(pl.multiple_of(start, 16), length)
 
-    own_half, other_half = rows_of(mx * h1, h1), rows_of((1 - mx) * h1, h1)
-
-    def piece1(offset):
-        return rows_of(mx * h1 + z_member(offset) * q1, q1)
-
-    def piece2(offset):
-        return rows_of(n1 + z_member(offset) * q2, q2)
-
-    def quarter2(which):
-        return rows_of(n1 + zi * q2 + which * e2, e2)
-
-    moves = [exchange(acc.at[:, pl.ds(give, lanes)], core_in, core_dev)]
-    each(0, 2, grad_input)
-    moves[0].wait()
-    summed = acc[:, pl.ds(keep, lanes)] + core_in[...]
-    total[...] = summed
-    stage[...] = summed.astype(BF16)
-
-    moves = [exchange(stage.at[other_half, :], x_in1, x_dev)]
-    moves += [exchange(stage.at[piece2(i), :], z_in2.at[i - 1], z_dev(i)) for i in (2, 1, 3)]
-    each(2, 5, grad_input)
-    relay(0)
-    for moved in moves:
-        moved.wait()
-    summed = total[own_half, :] + x_in1[...].astype(F32)
-    total[own_half, :] = summed
-    stage[own_half, :] = summed.astype(BF16)
-    summed = total[piece2(0), :]
-    for i in range(3):
-        summed = summed + z_in2[i].astype(F32)
-    total[piece2(0), :] = summed
-    stage[piece2(0), :] = summed.astype(BF16)
-
-    moves = [exchange(stage.at[piece1(i), :], z_in1.at[i - 1], z_dev(i)) for i in (2, 1, 3)]
-    moves += [exchange(stage.at[quarter2(1 - mx), :], x_in2, x_dev)]
-    each(5, CHUNKS, grad_input)
-    relay(1)
-    for moved in moves:
-        moved.wait()
-    summed = total[piece1(0), :]
-    for i in range(3):
-        summed = summed + z_in1[i].astype(F32)
-    slots[member, 0:q1, :] = summed.astype(BF16)
-    slots[member, q1 : q1 + e2, :] = (total[quarter2(mx), :] + x_in2[...].astype(F32)).astype(BF16)
-
-    moves = [exchange(slots.at[member], slots.at[member], m_dev(i)) for i in range(1, members)]
-    relay(2)
-    for moved in moves:
-        moved.wait()
-    summed = slots[0].astype(F32)
-    for i in range(1, members):
-        summed = summed + slots[i].astype(F32)
-    summed = (summed * scale).astype(BF16)
-    mine = pl.ds(keep, lanes)
-    full[piece1(0), mine] = summed[0:q1]
-    full[quarter2(mx), mine] = summed[q1 : q1 + e2]
-
-    def spread(rows, device):
+    def half_of(which, part_x):
+        return rows_of(bases[which] + part_x * half, half)
+
+    def piece_of(which, offset):
+        return rows_of(bases[which] + mx * half + z_member(offset) * piece, piece)
+
+    def spread(name, rows, device):
         place = full.at[rows, mine]
-        return exchange(place, place, device)
-
-    moves = [spread(piece1(0), z_dev(i)) for i in (2, 1, 3)] + [spread(quarter2(mx), x_dev)]
-    relay(3)
-    each(HALF, CHUNKS, output)
-    for moved in moves:
-        moved.wait()
-    moves = [spread(own_half, x_dev)] + [spread(piece2(0), z_dev(i)) for i in (2, 1, 3)]
-    shared = [spread(own_half, core_dev), spread(piece2(0), core_dev)]
-    each(0, HALF, output)
-    for moved in moves:
-        moved.wait()
-    shared += [spread(other_half, core_dev)] + [spread(piece2(i), core_dev) for i in (1, 2, 3)]
-    for moved in shared:
-        moved.wait()
+        exchange(name, place, place, device)
+
+    def to_core(which):
+        rows = rows_of(bases[which], block)
+        exchange(("core", which), acc.at[rows, pl.ds(give, lanes)], core_in.at[rows, :], core_dev)
+
+    def to_x(which):
+        landed(("core", which))
+        rows = rows_of(bases[which], block)
+        summed = acc[rows, mine] + core_in[rows, :]
+        total[rows, :] = summed
+        stage[rows, :] = summed.astype(BF16)
+        exchange(("x", which), stage.at[half_of(which, 1 - mx), :], x_in.at[which], x_dev)
+
+    def to_z(which):
+        landed(("x", which))
+        rows = half_of(which, mx)
+        summed = total[rows, :] + x_in[which].astype(F32)
+        total[rows, :] = summed
+        stage[rows, :] = summed.astype(BF16)
+        for offset in (2, 1, 3):
+            exchange(
+                ("z", which), stage.at[piece_of(which, offset), :], z_in.at[which, offset - 1],
+                z_dev(offset),
+            )
+
+    def to_y(which):
+        landed(("z", which))
+        summed = total[piece_of(which, 0), :]
+        for offset in range(3):
+            summed = summed + z_in[which, offset].astype(F32)
+        slots[which, member] = summed.astype(BF16)
+        place = slots.at[which, member]
+        for offset in range(1, members):
+            exchange(("y", which), place, place, m_dev(offset))
+
+    def back_z(which):
+        landed(("y", which))
+        summed = slots[which, 0].astype(F32)
+        for other in range(1, members):
+            summed = summed + slots[which, other].astype(F32)
+        full[piece_of(which, 0), mine] = (summed * scale).astype(BF16)
+        for offset in (2, 1, 3):
+            spread(("backz", which), piece_of(which, 0), z_dev(offset))
+        spread(("backx", which), piece_of(which, 0), x_dev)
+
+    def back_x(which):
+        landed(("backz", which))
+        for offset in (2, 3, 1):
+            spread(("backx", which), piece_of(which, offset), x_dev)
+        spread(("last", which), half_of(which, mx), core_dev)
+
+    def back_core(which):
+        landed(("backx", which))
+        spread(("last", which), half_of(which, 1 - mx), core_dev)
+
+    def fill_in(index):
+        receive(index)
+        backward(index, lambda which: None)
+
+        @pl.when(index >= 1)
+        def _():
+            grad_input(index - 1)
+
+    each(0, CHUNKS - 1, fill_in)
+    receive(CHUNKS - 1)
+
+    @pl.when(frame == 3)
+    def _():
+        def late(index):
+            rows = pl.ds(pl.multiple_of(index * size, size), size)
+            relay_last(index)
+            act_t = a2[rows, :].T
+            add_temporal(1, act_t, c1[rows, :])
+            add_temporal(2, act_t, cot[rows, :])
+
+        each(HALF, CHUNKS, late)
+
+    backward(CHUNKS - 1, to_core)
+
+    later = []
+    for which in range(4):
+        later += [
+            (0.5 + 0.6 * which, to_x, which), (5.6 + 2.1 * which, to_z, which),
+            (10.0 + 2.1 * which, to_y, which), (12.8 + 2.1 * which, back_z, which),
+            (17.2 + 2.1 * which, back_x, which), (20.0 + 2.1 * which, back_core, which),
+        ]
+    for index, when in GRAD_INPUT_AT:
+        later.append((when, grad_input, CHUNKS - 1 - index))
+    for index, when in enumerate(RELAY_AT):
+        later.append((when, relay_first, index))
+    for index, when in enumerate(LAST_AT):
+        later.append((when, relay_last, HALF - 1 - index))
+    for index, when in enumerate(HELD_AT):
+        later.append((when, held, CHUNKS - HOLD + index))
+    for when, start, stop in OUTPUT_AT:
+        later.append((when, lambda span: each(span[0], span[1], output), (start, stop)))
+    for _, action, argument in sorted(later, key=lambda entry: entry[0]):
+        action(argument)
+    for which in range(4):
+        landed(("last", which))
+
+    def written(index):
+        pltpu.make_async_copy(chunk(gin, index), chunk(gin_hbm, index), gin_sem.at[index]).wait()
+        pltpu.make_async_copy(chunk(out, index), chunk(out_hbm, index), out_sem.at[index]).wait()
+
+    each(0, CHUNKS, written)
 
     @pl.when(frame == 0)
     def _():
         each(0, HALF, lambda i: left(i, rc_sem))
-        each(0, HALF, lambda i: left(i, ra_sem))
+        each(0, VIA, lambda i: left(i, ra_sem))
         each(0, CHUNKS, lambda i: left(i, ay_sem))
         each(0, CHUNKS, lambda i: left(i, az_sem))
 
     @pl.when(frame == 1)
     def _():
         each(0, CHUNKS, lambda i: left(i, cy_sem))
-        each(0, HALF, lambda i: left(i, ay_sem))
+        each(0, VIA, lambda i: left(i, ay_sem))
         each(0, CHUNKS, lambda i: left(i, az_sem))
 
     @pl.when(frame == 2)
@@ -412,7 +470,41 @@
     def _():
         each(0, CHUNKS, lambda i: left(i, cy_sem))
         each(0, CHUNKS, lambda i: left(i, cz_sem))
-        each(HALF, CHUNKS, lambda i: left(i, ra_sem))
+        each(VIA, CHUNKS, lambda i: left(i, ra_sem))
+
+
+def finish_kernel(
+    out_in, gin_in, grads_in, out_hbm, gin_hbm, spatial_hbm, temporal_hbm,
+    out, gin, grads, wide, in_sem, out_sem,
+):
+    rows = out.shape[0] // 4
+    block = grads.shape[0] // 4
+    loads, stores = [], []
+
+    def start(moves, source, dest, sems):
+        moves.append(pltpu.make_async_copy(source, dest, sems.at[len(moves)]))
+        moves[-1].start()
+
+    parts = [pl.ds(part * block, block) for part in range(4)]
+    slabs = [pl.ds(part * rows, rows) for part in range(4)]
+    for part in parts:
+        start(loads, grads_in.at[part, :], grads.at[part, :], in_sem)
+    for source, dest in ((out_in, out), (gin_in, gin)):
+        for slab in slabs:
+            start(loads, source.at[slab, :], dest.at[slab, :], in_sem)
+    for index, part in enumerate(parts):
+        loads[index].wait()
+        wide[part, :] = grads[part, :].astype(F32)
+        target = spatial_hbm.at[part, :] if index < 3 else temporal_hbm
+        start(stores, wide.at[part, :], target, out_sem)
+    index = 4
+    for source, dest in ((out, out_hbm), (gin, gin_hbm)):
+        for slab in slabs:
+            loads[index].wait()
+            index += 1
+            start(stores, source.at[slab, :], dest.at[slab, :], out_sem)
+    for move in stores:
+        move.wait()
 
 
 def local(frames_in, spatial_weight, temporal_weight, cotangent):
@@ -429,10 +521,9 @@
     scale = 1.0 / math.sqrt(slab_rows * sp_count * dp_count * width)
 
     count = 12 * channels
-    h1, q1 = count // 3, count // 12
-    q2 = count // 12
-    e2 = q2 // 2
-    exchanges = 23 + members - 1
+    block = 3 * channels
+    half, piece = block // 2, block // 8
+    exchanges = 4 * (14 + members - 1)
     frame = jax.ShapeDtypeStruct((cells, channels), BF16)
     slab = pltpu.VMEM((cells, channels), BF16)
     padded = pltpu.VMEM((cells + 2 * width, 3 * channels), BF16)
@@ -442,27 +533,25 @@
         functools.partial(block_kernel, width, members, scale),
         out_shape=(frame, frame, jax.ShapeDtypeStruct((count, channels), BF16)),
         in_specs=[hbm, hbm, vmem, vmem],
-        out_specs=(vmem, vmem, vmem),
-        scratch_shapes=[slab] * 7
+        out_specs=(hbm, hbm, vmem),
+        scratch_shapes=[slab] * 9
         + [
             pltpu.VMEM((cells, channels), F32),
             padded,
             padded,
-            pltpu.VMEM((3, 3 * channels, channels), BF16),
+            pltpu.VMEM((3, block, channels), BF16),
             pltpu.VMEM((3, channels, channels), BF16),
             pltpu.VMEM((size, channels), F32),
             pltpu.VMEM((count, channels), F32),
             pltpu.VMEM((count, lanes), F32),
             pltpu.VMEM((count, lanes), F32),
             pltpu.VMEM((count, lanes), BF16),
-            pltpu.VMEM((h1, lanes), BF16),
-            pltpu.VMEM((e2, lanes), BF16),
-            pltpu.VMEM((3, q1, lanes), BF16),
-            pltpu.VMEM((3, q2, lanes), BF16),
-            pltpu.VMEM((members, q1 + e2, lanes), BF16),
+            pltpu.VMEM((4, half, lanes), BF16),
+            pltpu.VMEM((4, 3, piece, lanes), BF16),
+            pltpu.VMEM((4, members, piece, lanes), BF16),
             pltpu.SemaphoreType.DMA((2,)),
         ]
-        + [pltpu.SemaphoreType.DMA((CHUNKS,))] * 10
+        + [pltpu.SemaphoreType.DMA((CHUNKS,))] * 12
         + [pltpu.SemaphoreType.DMA((exchanges,))] * 2,
         compiler_params=pltpu.CompilerParams(
             collective_id=0, has_side_effects=True, vmem_limit_bytes=VMEM_LIMIT
@@ -475,9 +564,28 @@
         name="video_block",
     )(x, cot, w3, temporal_weight)
 
-    grads = grads.astype(F32)
-    grad_spatial = grads[: 9 * channels].reshape(3, 3, channels, channels)
-    grad_temporal = grads[9 * channels :].reshape(3, channels, channels)
+    block_out, grad_in, grad_spatial, grad_temporal = pl.pallas_call(
+        finish_kernel,
+        out_shape=(
+            frame, frame,
+            jax.ShapeDtypeStruct((9 * channels, channels), F32),
+            jax.ShapeDtypeStruct((3 * channels, channels), F32),
+        ),
+        in_specs=[hbm] * 3,
+        out_specs=(hbm,) * 4,
+        scratch_shapes=[
+            slab,
+            slab,
+            pltpu.VMEM((count, channels), BF16),
+            pltpu.VMEM((count, channels), F32),
+            pltpu.SemaphoreType.DMA((12,)),
+            pltpu.SemaphoreType.DMA((12,)),
+        ],
+        compiler_params=pltpu.CompilerParams(vmem_limit_bytes=VMEM_LIMIT),
+        name="finish",
+    )(block_out, grad_in, grads)
+    grad_spatial = grad_spatial.reshape(3, 3, channels, channels)
+    grad_temporal = grad_temporal.reshape(3, channels, channels)
     return (
         block_out.reshape(frames_in.shape),
         grad_in.reshape(frames_in.shape),

time: 114 us -> 103 us (0.904)
  local copies, waits for them, and re-layouts: 8.16 us -> 0 us
  Pallas kernels: 105 us -> 102 us
    pallas_call x1, Pallas kernels: 105 us -> 96.4 us  [local(): pl.pallas_call(functools.partial(block_kernel, width, members, scale), ou...]
    pallas_call x0 -> x1, Pallas kernels: none -> 5.28 us  [local(): pl.pallas_call(finish_kernel, out_shape=(frame, frame, jax.ShapeDtypeStru...]
    unnamed x8 -> x0, local copies, waits for them, and re-layouts: 4.53 us -> none
    slice x2 -> x0, local copies, waits for them, and re-layouts: 3.64 us -> none  [the longest x1 2.05 us: local(): grad_temporal = grads[9 * channels:].reshape(3, channels, channels)]
where the time goes in v2:
time: 103 us; the launch traced here: 102 us
  Pallas kernels  102 us (99%)
    pallas_call x1, Pallas kernels, local(): pl.pallas_call(functools.partial(block_kernel, width, members, scale), ou...  96.4 us
    pallas_call x1, Pallas kernels, local(): pl.pallas_call(finish_kernel, out_shape=(frame, frame, jax.ShapeDtypeStru...  5.28 us

profile of v2, /device:TPU:0, one launch (start us, length us, event | category | flops | bytes accessed | tf_op | source)
XLA Modules:
  0.0 102.3 jit_solution(70946007058401921)
XLA Ops:
  0.6 96.4 %video_block.1 = (bf16[4096,256]{1,0:T(8,128)(2,1)}, bf16[4096,256]{1,0:T(8,128)(2,1)}, bf16[3072,256]{1,0:T(8,128)(2,1)}) custom-call(bf16[4096,256]{1,0:T(8,128)(2,1)} %bitcast.8, bf16[4096,256]{1,0:T(8,128)(2,1)} %bitcast.9, bf16[3,768,256]{2,1,0:T(8,128)(2,1)} %bitcast.12, bf16[3,256,256]{2,1,0:T(8,128)(2,1)} %tw_ref.1), custom_call_target="tpu_custom_call" | custom-call | flops 19327352832 | bytes 16777216 | tf_op jit(solution)/shard_map/video_block/pallas_call | solution.py:532
  97.0 5.3 %finish.1 = (bf16[4096,256]{1,0:T(8,128)(2,1)}, bf16[4096,256]{1,0:T(8,128)(2,1)}, f32[2304,256]{1,0:T(8,128)}, f32[768,256]{1,0:T(8,128)}) custom-call(bf16[4096,256]{1,0:T(8,128)(2,1)} %get-tuple-element.11.out_in, bf16[4096,256]{1,0:T(8,128)(2,1)} %get-tuple-element.12.gin_in, bf16[3072,256]{1,0:T(8,128)(2,1)} %get-tuple-element.13.grads_in), custom_call_target="tpu_custom_call" | custom-call | tf_op jit(solution)/shard_map/finish/pallas_call | solution.py:567

commit v3 on v2

--- a/solution.py
+++ b/solution.py
@@ -14,12 +14,16 @@
 LEAD = CHUNKS // 8
 VIA = 2
 HOLD = 1
+Z_FIRST = (0,)
+SPLIT = 1
+X_FIRST_AT = ((0.5, 0.6), (3.5, 2.1), (8.0, 2.1), (10.8, 2.1), (15.2, 2.1), (18.0, 2.1))
+Z_FIRST_AT = ((0.5, 0.6), (8.0, 0.6), (11.0, 0.6), (13.8, 0.6), (18.3, 2.1), (20.9, 2.1))
 HELD_AT = (19.3,)
 GRAD_INPUT_AT = ((1, 3.0), (0, 3.1))
 RELAY_AT = (2.5, 13.5)
-LAST_AT = (19.5, 19.6)
+LAST_AT = (14.5, 19.6)
 OUTPUT_AT = ((20.5, 4, 5), (20.6, 5, 6), (22.5, 6, 7), (28.0, 0, 2), (28.1, 7, 8), (28.2, 3, 4), (28.3, 2, 3))
-VMEM_LIMIT = 58 * 1024 * 1024
+VMEM_LIMIT = 48 * 1024 * 1024
 MESH = pl.DeviceIdType.MESH
 F32 = jnp.float32
 BF16 = jnp.bfloat16
@@ -47,12 +51,12 @@
 
 def block_kernel(
     width, members, scale,
-    x_hbm, cot_hbm, w_ref, tw_ref,
-    out_hbm, gin_hbm, full,
-    x, cot, c1, c2, a1, a2, act, out, gin, slope, x3, g3, wf, wt, part, acc,
+    x_hbm, cot_hbm, w_hbm, tw_hbm,
+    out, gin, full,
+    x, cot, c1, c2, a1, a2, act, slope, x3, g3, w_ref, tw_ref, wf, wt, part, acc,
     core_in, total, stage, x_in, z_in, slots,
     load_sem, c1_sem, c2_sem, a1_sem, a2_sem, cy_sem, cz_sem, ay_sem, az_sem, rc_sem, ra_sem,
-    out_sem, gin_sem, red_send, red_recv,
+    red_send, red_recv,
 ):
     dp = lax.axis_index("dp")
     sp = lax.axis_index("sp")
@@ -115,8 +119,10 @@
 
     x_load = pltpu.make_async_copy(x_hbm, x, load_sem.at[0])
     cot_load = pltpu.make_async_copy(cot_hbm, cot, load_sem.at[1])
-    x_load.start()
-    cot_load.start()
+    w_load = pltpu.make_async_copy(w_hbm, w_ref, load_sem.at[2])
+    tw_load = pltpu.make_async_copy(tw_hbm, tw_ref, load_sem.at[3])
+    for load in (x_load, w_load, tw_load, cot_load):
+        load.start()
 
     barrier = pltpu.get_barrier_semaphore()
     greeted = [core_dev, x_dev] + [z_dev(i) for i in (1, 2, 3)] + [m_dev(i) for i in range(1, members)]
@@ -142,6 +148,7 @@
     zero_edges(x3, width)
     zero_edges(g3, width)
     x_load.wait()
+    w_load.wait()
 
     def forward(step):
         @pl.when(step < CHUNKS)
@@ -188,6 +195,7 @@
     def _():
         each(0, HALF, lambda i: send(act, a2, HALF - 1 - i, az_sem, a2_sem, t_dev))
 
+    tw_load.wait()
     for tap in range(3):
         wt[tap] = tw_ref[tap].T
         for side in range(3):
@@ -265,7 +273,6 @@
         for tap in range(3):
             total_in = total_in + mm(g3[pl.ds(base + tap * width, size), :], wf[tap])
         gin[pl.ds(base, size), :] = total_in.astype(BF16)
-        pltpu.make_async_copy(chunk(gin, index), chunk(gin_hbm, index), gin_sem.at[index]).start()
 
     def output(index):
         rows = pl.ds(pl.multiple_of(index * size, size), size)
@@ -290,7 +297,6 @@
 
         temporal = part[...].astype(BF16).astype(F32)
         out[rows, :] = (x[rows, :].astype(F32) + temporal).astype(BF16)
-        pltpu.make_async_copy(chunk(out, index), chunk(out_hbm, index), out_sem.at[index]).start()
 
     def relay_first(index):
         @pl.when(frame == 0)
@@ -309,11 +315,16 @@
         def _():
             send(act, a1, index, ay_sem, a1_sem, y_dev)
 
-    half, piece = block // 2, block // 8
+    span = block // SPLIT
+    half, piece = span // 2, span // 8
     keep = pl.multiple_of(core * lanes, lanes)
     give = pl.multiple_of((1 - core) * lanes, lanes)
     mine = pl.ds(keep, lanes)
-    bases = [gt_base] + [tap * block for tap in range(3)]
+    bases = [
+        start + part_of * span
+        for start in [gt_base] + [tap * block for tap in range(3)]
+        for part_of in range(SPLIT)
+    ]
     used = []
     moving = {}
 
@@ -335,41 +346,71 @@
         return rows_of(bases[which] + part_x * half, half)
 
     def piece_of(which, offset):
+        if which in Z_FIRST:
+            return rows_of(bases[which] + z_member(offset) * 2 * piece + mx * piece, piece)
         return rows_of(bases[which] + mx * half + z_member(offset) * piece, piece)
+
+    def pair_of(which, offset):
+        return rows_of(bases[which] + z_member(offset) * 2 * piece, 2 * piece)
 
     def spread(name, rows, device):
         place = full.at[rows, mine]
         exchange(name, place, place, device)
 
     def to_core(which):
-        rows = rows_of(bases[which], block)
+        rows = rows_of(bases[which], span)
         exchange(("core", which), acc.at[rows, pl.ds(give, lanes)], core_in.at[rows, :], core_dev)
 
-    def to_x(which):
+    def to_first(which):
         landed(("core", which))
-        rows = rows_of(bases[which], block)
+        rows = rows_of(bases[which], span)
         summed = acc[rows, mine] + core_in[rows, :]
         total[rows, :] = summed
         stage[rows, :] = summed.astype(BF16)
-        exchange(("x", which), stage.at[half_of(which, 1 - mx), :], x_in.at[which], x_dev)
-
-    def to_z(which):
-        landed(("x", which))
-        rows = half_of(which, mx)
-        summed = total[rows, :] + x_in[which].astype(F32)
+        if which in Z_FIRST:
+            for offset in (2, 1, 3):
+                exchange(
+                    ("first", which), stage.at[pair_of(which, offset), :],
+                    z_in.at[which, offset - 1], z_dev(offset),
+                )
+        else:
+            exchange(
+                ("first", which), stage.at[half_of(which, 1 - mx), :],
+                x_in.at[which], x_dev,
+            )
+
+    def to_second(which):
+        landed(("first", which))
+        if which in Z_FIRST:
+            rows = pair_of(which, 0)
+            summed = total[rows, :]
+            for offset in range(3):
+                summed = summed + z_in[which, offset].astype(F32)
+        else:
+            rows = half_of(which, mx)
+            summed = total[rows, :] + x_in[which].astype(F32)
         total[rows, :] = summed
         stage[rows, :] = summed.astype(BF16)
-        for offset in (2, 1, 3):
+        if which in Z_FIRST:
+            other = rows_of(bases[which] + zi * 2 * piece + (1 - mx) * piece, piece)
             exchange(
-                ("z", which), stage.at[piece_of(which, offset), :], z_in.at[which, offset - 1],
-                z_dev(offset),
+                ("second", which), stage.at[other, :], x_in.at[which, 0:piece, :], x_dev
             )
+        else:
+            for offset in (2, 1, 3):
+                exchange(
+                    ("second", which), stage.at[piece_of(which, offset), :],
+                    z_in.at[which, offset - 1, 0:piece, :], z_dev(offset),
+                )
 
     def to_y(which):
-        landed(("z", which))
+        landed(("second", which))
         summed = total[piece_of(which, 0), :]
-        for offset in range(3):
-            summed = summed + z_in[which, offset].astype(F32)
+        if which in Z_FIRST:
+            summed = summed + x_in[which, 0:piece, :].astype(F32)
+        else:
+            for offset in range(3):
+                summed = summed + z_in[which, offset, 0:piece, :].astype(F32)
         slots[which, member] = summed.astype(BF16)
         place = slots.at[which, member]
         for offset in range(1, members):
@@ -389,11 +430,15 @@
         landed(("backz", which))
         for offset in (2, 3, 1):
             spread(("backx", which), piece_of(which, offset), x_dev)
-        spread(("last", which), half_of(which, mx), core_dev)
+        if which not in Z_FIRST:
+            spread(("last", which), half_of(which, mx), core_dev)
 
     def back_core(which):
         landed(("backx", which))
-        spread(("last", which), half_of(which, 1 - mx), core_dev)
+        if which in Z_FIRST:
+            spread(("last", which), rows_of(bases[which], span), core_dev)
+        else:
+            spread(("last", which), half_of(which, 1 - mx), core_dev)
 
     def fill_in(index):
         receive(index)
@@ -417,15 +462,18 @@
 
         each(HALF, CHUNKS, late)
 
-    backward(CHUNKS - 1, to_core)
+    def all_to_core(which):
+        for part_of in range(SPLIT):
+            to_core(which * SPLIT + part_of)
+
+    backward(CHUNKS - 1, all_to_core)
 
     later = []
-    for which in range(4):
-        later += [
-            (0.5 + 0.6 * which, to_x, which), (5.6 + 2.1 * which, to_z, which),
-            (10.0 + 2.1 * which, to_y, which), (12.8 + 2.1 * which, back_z, which),
-            (17.2 + 2.1 * which, back_x, which), (20.0 + 2.1 * which, back_core, which),
-        ]
+    actions = (to_first, to_second, to_y, back_z, back_x, back_core)
+    for which in range(4 * SPLIT):
+        times = Z_FIRST_AT if which in Z_FIRST else X_FIRST_AT
+        for action, (when, stride) in zip(actions, times):
+            later.append((when + stride * which / SPLIT, action, which))
     for index, when in GRAD_INPUT_AT:
         later.append((when, grad_input, CHUNKS - 1 - index))
     for index, when in enumerate(RELAY_AT):
@@ -438,14 +486,8 @@
         later.append((when, lambda span: each(span[0], span[1], output), (start, stop)))
     for _, action, argument in sorted(later, key=lambda entry: entry[0]):
         action(argument)
-    for which in range(4):
+    for which in range(4 * SPLIT):
         landed(("last", which))
-
-    def written(index):
-        pltpu.make_async_copy(chunk(gin, index), chunk(gin_hbm, index), gin_sem.at[index]).wait()
-        pltpu.make_async_copy(chunk(out, index), chunk(out_hbm, index), out_sem.at[index]).wait()
-
-    each(0, CHUNKS, written)
 
     @pl.when(frame == 0)
     def _():
@@ -474,35 +516,21 @@
 
 
 def finish_kernel(
-    out_in, gin_in, grads_in, out_hbm, gin_hbm, spatial_hbm, temporal_hbm,
-    out, gin, grads, wide, in_sem, out_sem,
+    out, gin, grads, out_hbm, gin_hbm, spatial_hbm, temporal_hbm, wide, sems
 ):
-    rows = out.shape[0] // 4
     block = grads.shape[0] // 4
-    loads, stores = [], []
-
-    def start(moves, source, dest, sems):
-        moves.append(pltpu.make_async_copy(source, dest, sems.at[len(moves)]))
-        moves[-1].start()
-
-    parts = [pl.ds(part * block, block) for part in range(4)]
-    slabs = [pl.ds(part * rows, rows) for part in range(4)]
-    for part in parts:
-        start(loads, grads_in.at[part, :], grads.at[part, :], in_sem)
-    for source, dest in ((out_in, out), (gin_in, gin)):
-        for slab in slabs:
-            start(loads, source.at[slab, :], dest.at[slab, :], in_sem)
-    for index, part in enumerate(parts):
-        loads[index].wait()
+    stores = []
+
+    def store(source, dest):
+        stores.append(pltpu.make_async_copy(source, dest, sems.at[len(stores)]))
+        stores[-1].start()
+
+    store(out, out_hbm)
+    store(gin, gin_hbm)
+    for index in range(4):
+        part = pl.ds(index * block, block)
         wide[part, :] = grads[part, :].astype(F32)
-        target = spatial_hbm.at[part, :] if index < 3 else temporal_hbm
-        start(stores, wide.at[part, :], target, out_sem)
-    index = 4
-    for source, dest in ((out, out_hbm), (gin, gin_hbm)):
-        for slab in slabs:
-            loads[index].wait()
-            index += 1
-            start(stores, source.at[slab, :], dest.at[slab, :], out_sem)
+        store(wide.at[part, :], spatial_hbm.at[part, :] if index < 3 else temporal_hbm)
     for move in stores:
         move.wait()
 
@@ -522,23 +550,26 @@
 
     count = 12 * channels
     block = 3 * channels
-    half, piece = block // 2, block // 8
-    exchanges = 4 * (14 + members - 1)
+    blocks = 4 * SPLIT
+    half, piece = block // SPLIT // 2, block // SPLIT // 8
+    exchanges = blocks * (14 + members - 1)
     frame = jax.ShapeDtypeStruct((cells, channels), BF16)
     slab = pltpu.VMEM((cells, channels), BF16)
     padded = pltpu.VMEM((cells + 2 * width, 3 * channels), BF16)
     vmem = pl.BlockSpec(memory_space=pltpu.VMEM)
-    hbm = pl.BlockSpec(memory_space=pl.ANY)
+    hbm = pl.BlockSpec(memory_space=pltpu.HBM)
     block_out, grad_in, grads = pl.pallas_call(
         functools.partial(block_kernel, width, members, scale),
-        out_shape=(frame, frame, jax.ShapeDtypeStruct((count, channels), BF16)),
-        in_specs=[hbm, hbm, vmem, vmem],
-        out_specs=(hbm, hbm, vmem),
-        scratch_shapes=[slab] * 9
+        out_shape=(slab, slab, pltpu.VMEM((count, channels), BF16)),
+        in_specs=[hbm] * 4,
+        out_specs=(vmem,) * 3,
+        scratch_shapes=[slab] * 7
         + [
             pltpu.VMEM((cells, channels), F32),
             padded,
             padded,
+            pltpu.VMEM((3, block, channels), BF16),
+            pltpu.VMEM((3, channels, channels), BF16),
             pltpu.VMEM((3, block, channels), BF16),
             pltpu.VMEM((3, channels, channels), BF16),
             pltpu.VMEM((size, channels), F32),
@@ -546,12 +577,12 @@
             pltpu.VMEM((count, lanes), F32),
             pltpu.VMEM((count, lanes), F32),
             pltpu.VMEM((count, lanes), BF16),
-            pltpu.VMEM((4, half, lanes), BF16),
-            pltpu.VMEM((4, 3, piece, lanes), BF16),
-            pltpu.VMEM((4, members, piece, lanes), BF16),
-            pltpu.SemaphoreType.DMA((2,)),
+            pltpu.VMEM((blocks, half, lanes), BF16),
+            pltpu.VMEM((blocks, 3, 2 * piece, lanes), BF16),
+            pltpu.VMEM((blocks, members, piece, lanes), BF16),
+            pltpu.SemaphoreType.DMA((4,)),
         ]
-        + [pltpu.SemaphoreType.DMA((CHUNKS,))] * 12
+        + [pltpu.SemaphoreType.DMA((CHUNKS,))] * 10
         + [pltpu.SemaphoreType.DMA((exchanges,))] * 2,
         compiler_params=pltpu.CompilerParams(
             collective_id=0, has_side_effects=True, vmem_limit_bytes=VMEM_LIMIT
@@ -571,17 +602,10 @@
             jax.ShapeDtypeStruct((9 * channels, channels), F32),
             jax.ShapeDtypeStruct((3 * channels, channels), F32),
         ),
-        in_specs=[hbm] * 3,
+        in_specs=[vmem] * 3,
         out_specs=(hbm,) * 4,
-        scratch_shapes=[
-            slab,
-            slab,
-            pltpu.VMEM((count, channels), BF16),
-            pltpu.VMEM((count, channels), F32),
-            pltpu.SemaphoreType.DMA((12,)),
-            pltpu.SemaphoreType.DMA((12,)),
-        ],
-        compiler_params=pltpu.CompilerParams(vmem_limit_bytes=VMEM_LIMIT),
+        scratch_shapes=[pltpu.VMEM((count, channels), F32), pltpu.SemaphoreType.DMA((6,))],
+        compiler_params=pltpu.CompilerParams(vmem_limit_bytes=16 * 1024 * 1024),
         name="finish",
     )(block_out, grad_in, grads)
     grad_spatial = grad_spatial.reshape(3, 3, channels, channels)

time: 103 us -> 96.9 us (0.941)
  Pallas kernels: 102 us -> 95.1 us
    pallas_call x1, Pallas kernels: 96.4 us -> 92.1 us  [local(): pl.pallas_call(functools.partial(block_kernel, width, members, scale), ou...]
    pallas_call x1, Pallas kernels: 5.28 us -> 3.02 us  [local(): pl.pallas_call(finish_kernel, out_shape=(frame, frame, jax.ShapeDtypeStru...]
where the time goes in v3:
time: 96.9 us; the launch traced here: 96.7 us
  Pallas kernels  95.1 us (98%)
  local copies, waits for them, and re-layouts  0.99 us (1%)
    pallas_call x1, Pallas kernels, local(): pl.pallas_call(functools.partial(block_kernel, width, members, scale), ou...  92.1 us
    pallas_call x1, Pallas kernels, local(): pl.pallas_call(finish_kernel, out_shape=(frame, frame, jax.ShapeDtypeStru...  3.02 us

profile of v3, /device:TPU:0, one launch (start us, length us, event | category | flops | bytes accessed | tf_op | source)
XLA Modules:
  0.0 96.7 jit_solution(17757900010604220579)
XLA Ops:
  0.6 0.0 copy-start
  0.6 1.0 %copy-done = bf16[3,256,256]{2,1,0:T(8,128)(2,1)S(1)} copy-done((bf16[3,256,256]{2,1,0:T(8,128)(2,1)S(1)}, bf16[3,256,256]{2,1,0:T(8,128)(2,1)}, u32[]{:S(2)}) %copy-start) | copy-done | bytes 393240
  1.6 92.1 %video_block.1 = (bf16[4096,256]{1,0:T(8,128)(2,1)S(1)}, bf16[4096,256]{1,0:T(8,128)(2,1)S(1)}, bf16[3072,256]{1,0:T(8,128)(2,1)S(1)}) custom-call(bf16[4096,256]{1,0:T(8,128)(2,1)} %bitcast.8, bf16[4096,256]{1,0:T(8,128)(2,1)} %bitcast.9, bf16[3,768,256]{2,1,0:T(8,128)(2,1)} %bitcast.12, bf16[3,256,256]{2,1,0:T(8,128)(2,1)S(1)} %copy-done), custom_call_target="tpu_custom_call" | custom-call | flops 19327352832 | bytes 16777216 | tf_op jit(solution)/shard_map/video_block/pallas_call | solution.py:561
  93.7 3.0 %finish.1 = (bf16[4096,256]{1,0:T(8,128)(2,1)}, bf16[4096,256]{1,0:T(8,128)(2,1)}, f32[2304,256]{1,0:T(8,128)}, f32[768,256]{1,0:T(8,128)}) custom-call(bf16[4096,256]{1,0:T(8,128)(2,1)S(1)} %get-tuple-element.11.out, bf16[4096,256]{1,0:T(8,128)(2,1)S(1)} %get-tuple-element.12.gin, bf16[3072,256]{1,0:T(8,128)(2,1)S(1)} %get-tuple-element.13.grads), custom_call_target="tpu_custom_call" | custom-call | tf_op jit(solution)/shard_map/finish/pallas_call | solution.py:598
Async XLA Ops:
  0.6 1.0 %copy-start = (bf16[3,256,256]{2,1,0:T(8,128)(2,1)S(1)}, bf16[3,256,256]{2,1,0:T(8,128)(2,1)}, u32[]{:S(2)}) copy-start(bf16[3,256,256]{2,1,0:T(8,128)(2,1)} %tw_hbm.1) | copy-start | bytes 1179652

commit v4 on v3

--- a/solution.py
+++ b/solution.py
@@ -12,7 +12,7 @@
 CHUNKS = 8
 HALF = CHUNKS // 2
 LEAD = CHUNKS // 8
-VIA = 2
+VIA = 3
 HOLD = 1
 Z_FIRST = (0,)
 SPLIT = 1
@@ -20,9 +20,12 @@
 Z_FIRST_AT = ((0.5, 0.6), (8.0, 0.6), (11.0, 0.6), (13.8, 0.6), (18.3, 2.1), (20.9, 2.1))
 HELD_AT = (19.3,)
 GRAD_INPUT_AT = ((1, 3.0), (0, 3.1))
-RELAY_AT = (2.5, 13.5)
-LAST_AT = (14.5, 19.6)
-OUTPUT_AT = ((20.5, 4, 5), (20.6, 5, 6), (22.5, 6, 7), (28.0, 0, 2), (28.1, 7, 8), (28.2, 3, 4), (28.3, 2, 3))
+RELAY_AT = (2.5, 13.5, 21.6)
+NOW = 2
+LAST_AT = (5.0, 17.2, 19.6)
+OWN_AT = 3.2
+OLD_AT = ((9.0, 4, 6), (11.5, 6, 8), (13.6, 0, 2), (15.9, 2, 3), (19.7, 3, 4))
+OUTPUT_AT = ((15.28, 4, 5), (17.38, 5, 6), (19.28, 6, 7), (21.28, 0, 1), (23.28, 7, 8), (28.1, 1, 2), (28.2, 3, 4), (28.3, 2, 3))
 VMEM_LIMIT = 48 * 1024 * 1024
 MESH = pl.DeviceIdType.MESH
 F32 = jnp.float32
@@ -274,29 +277,36 @@
             total_in = total_in + mm(g3[pl.ds(base + tap * width, size), :], wf[tap])
         gin[pl.ds(base, size), :] = total_in.astype(BF16)
 
+    def own_term(index):
+        rows = pl.ds(pl.multiple_of(index * size, size), size)
+        slope[rows, :] = mm(act[rows, :], tw_ref[0])
+
+    def old_term(index):
+        rows = pl.ds(pl.multiple_of(index * size, size), size)
+
+        @pl.when((frame == 2) | ((frame == 3) & (index < VIA)))
+        def _():
+            arrived(a2, index, a2_sem)
+
+        @pl.when(frame >= 2)
+        def _():
+            slope[rows, :] += mm(a2[rows, :], tw_ref[2])
+
     def output(index):
         rows = pl.ds(pl.multiple_of(index * size, size), size)
 
+        def write(temporal):
+            temporal = temporal.astype(BF16).astype(F32)
+            out[rows, :] = (x[rows, :].astype(F32) + temporal).astype(BF16)
+
+        @pl.when(frame == 0)
+        def _():
+            write(slope[rows, :])
+
         @pl.when(frame >= 1)
         def _():
             arrived(a1, index, a1_sem)
-
-        @pl.when((frame == 2) | ((frame == 3) & (index < VIA)))
-        def _():
-            arrived(a2, index, a2_sem)
-
-        part[...] = mm(act[rows, :], tw_ref[0])
-
-        @pl.when(frame >= 1)
-        def _():
-            part[...] += mm(a1[rows, :], tw_ref[1])
-
-        @pl.when(frame >= 2)
-        def _():
-            part[...] += mm(a2[rows, :], tw_ref[2])
-
-        temporal = part[...].astype(BF16).astype(F32)
-        out[rows, :] = (x[rows, :].astype(F32) + temporal).astype(BF16)
+            write(slope[rows, :] + mm(a1[rows, :], tw_ref[1]))
 
     def relay_first(index):
         @pl.when(frame == 0)
@@ -307,7 +317,8 @@
     def relay_last(index):
         @pl.when(frame == 3)
         def _():
-            arrived(a2, index, a2_sem)
+            if index < HALF:
+                arrived(a2, index, a2_sem)
             send(a2, a1, index, ra_sem, a1_sem, y_dev)
 
     def held(index):
@@ -448,6 +459,8 @@
         def _():
             grad_input(index - 1)
 
+        own_term(index)
+
     each(0, CHUNKS - 1, fill_in)
     receive(CHUNKS - 1)
 
@@ -455,7 +468,12 @@
     def _():
         def late(index):
             rows = pl.ds(pl.multiple_of(index * size, size), size)
-            relay_last(index)
+            arrived(a2, index, a2_sem)
+
+            @pl.when(index < HALF + NOW)
+            def _():
+                send(a2, a1, index, ra_sem, a1_sem, y_dev)
+
             act_t = a2[rows, :].T
             add_temporal(1, act_t, c1[rows, :])
             add_temporal(2, act_t, cot[rows, :])
@@ -476,10 +494,14 @@
             later.append((when + stride * which / SPLIT, action, which))
     for index, when in GRAD_INPUT_AT:
         later.append((when, grad_input, CHUNKS - 1 - index))
+    later.append((OWN_AT, own_term, CHUNKS - 1))
+    for when, start, stop in OLD_AT:
+        later.append((when, lambda span: each(span[0], span[1], old_term), (start, stop)))
     for index, when in enumerate(RELAY_AT):
         later.append((when, relay_first, index))
-    for index, when in enumerate(LAST_AT):
-        later.append((when, relay_last, HALF - 1 - index))
+    waiting = [*range(HALF + NOW, CHUNKS), *range(HALF - 1, VIA - 1, -1)]
+    for index, when in zip(waiting, LAST_AT):
+        later.append((when, relay_last, index))
     for index, when in enumerate(HELD_AT):
         later.append((when, held, CHUNKS - HOLD + index))
     for when, start, stop in OUTPUT_AT:

time: 96.9 us -> 95.3 us (0.983)
  Pallas kernels: 95.1 us -> 93.5 us
    pallas_call x1, Pallas kernels: 92.1 us -> 90.5 us  [local(): pl.pallas_call(functools.partial(block_kernel, width, members, scale), ou...]
where the time goes in v4:
time: 95.3 us; the launch traced here: 95.2 us
  Pallas kernels  93.5 us (98%)
  local copies, waits for them, and re-layouts  0.99 us (1%)
    pallas_call x1, Pallas kernels, local(): pl.pallas_call(functools.partial(block_kernel, width, members, scale), ou...  90.5 us
    pallas_call x1, Pallas kernels, local(): pl.pallas_call(finish_kernel, out_shape=(frame, frame, jax.ShapeDtypeStru...  3.02 us

profile of v4, /device:TPU:0, one launch (start us, length us, event | category | flops | bytes accessed | tf_op | source)
XLA Modules:
  0.0 95.2 jit_solution(4708541636719726771)
XLA Ops:
  0.6 0.0 copy-start
  0.6 1.0 %copy-done = bf16[3,256,256]{2,1,0:T(8,128)(2,1)S(1)} copy-done((bf16[3,256,256]{2,1,0:T(8,128)(2,1)S(1)}, bf16[3,256,256]{2,1,0:T(8,128)(2,1)}, u32[]{:S(2)}) %copy-start) | copy-done | bytes 393240
  1.6 90.5 %video_block.1 = (bf16[4096,256]{1,0:T(8,128)(2,1)S(1)}, bf16[4096,256]{1,0:T(8,128)(2,1)S(1)}, bf16[3072,256]{1,0:T(8,128)(2,1)S(1)}) custom-call(bf16[4096,256]{1,0:T(8,128)(2,1)} %bitcast.8, bf16[4096,256]{1,0:T(8,128)(2,1)} %bitcast.9, bf16[3,768,256]{2,1,0:T(8,128)(2,1)} %bitcast.12, bf16[3,256,256]{2,1,0:T(8,128)(2,1)S(1)} %copy-done), custom_call_target="tpu_custom_call" | custom-call | flops 19327352832 | bytes 16777216 | tf_op jit(solution)/shard_map/video_block/pallas_call | solution.py:583
  92.1 3.0 %finish.1 = (bf16[4096,256]{1,0:T(8,128)(2,1)}, bf16[4096,256]{1,0:T(8,128)(2,1)}, f32[2304,256]{1,0:T(8,128)}, f32[768,256]{1,0:T(8,128)}) custom-call(bf16[4096,256]{1,0:T(8,128)(2,1)S(1)} %get-tuple-element.11.out, bf16[4096,256]{1,0:T(8,128)(2,1)S(1)} %get-tuple-element.12.gin, bf16[3072,256]{1,0:T(8,128)(2,1)S(1)} %get-tuple-element.13.grads), custom_call_target="tpu_custom_call" | custom-call | tf_op jit(solution)/shard_map/finish/pallas_call | solution.py:620
Async XLA Ops:
  0.6 1.0 %copy-start = (bf16[3,256,256]{2,1,0:T(8,128)(2,1)S(1)}, bf16[3,256,256]{2,1,0:T(8,128)(2,1)}, u32[]{:S(2)}) copy-start(bf16[3,256,256]{2,1,0:T(8,128)(2,1)} %tw_hbm.1) | copy-start | bytes 1179652

commit v5 on v4

--- a/solution.py
+++ b/solution.py
@@ -26,7 +26,7 @@
 OWN_AT = 3.2
 OLD_AT = ((9.0, 4, 6), (11.5, 6, 8), (13.6, 0, 2), (15.9, 2, 3), (19.7, 3, 4))
 OUTPUT_AT = ((15.28, 4, 5), (17.38, 5, 6), (19.28, 6, 7), (21.28, 0, 1), (23.28, 7, 8), (28.1, 1, 2), (28.2, 3, 4), (28.3, 2, 3))
-VMEM_LIMIT = 48 * 1024 * 1024
+VMEM_LIMIT = 50 * 1024 * 1024
 MESH = pl.DeviceIdType.MESH
 F32 = jnp.float32
 BF16 = jnp.bfloat16
@@ -56,7 +56,7 @@
     width, members, scale,
     x_hbm, cot_hbm, w_hbm, tw_hbm,
     out, gin, full,
-    x, cot, c1, c2, a1, a2, act, slope, x3, g3, w_ref, tw_ref, wf, wt, part, acc,
+    x, cot, c1, c2, a1, a2, act, slope, x3, g3, w_ref, tw_ref, wf, wt, part, act_last, x_last, acc,
     core_in, total, stage, x_in, z_in, slots,
     load_sem, c1_sem, c2_sem, a1_sem, a2_sem, cy_sem, cz_sem, ay_sem, az_sem, rc_sem, ra_sem,
     red_send, red_recv,
@@ -238,13 +238,18 @@
             c2[rows, :] = (mm(c1[rows, :], wt[1]) + mm(cot[rows, :], wt[2])).astype(BF16)
             send(c2, c1, index, cz_sem, c1_sem, t_dev)
 
-    def backward(index, finish):
+    def own_gradient(index):
+        rows = pl.ds(pl.multiple_of(index * size, size), size)
+        act_t = act[rows, :].T
+        part[...] = mm(cot[rows, :], wt[0])
+        add_temporal(0, act_t, cot[rows, :])
+        return act_t
+
+    def backward(index, finish, last=False):
         base = pl.multiple_of(index * size, size)
         rows = pl.ds(base, size)
         early = index < HALF
-        act_t = act[rows, :].T
-        part[...] = mm(cot[rows, :], wt[0])
-        add_temporal(0, act_t, cot[rows, :])
+        act_t = act_last[...] if last else own_gradient(index)
 
         @pl.when((frame == 0) | (frame == 2) | ((frame == 1) & early))
         def _():
@@ -266,8 +271,8 @@
         store_shifted(g3, pl.multiple_of(width + base, width), grad_pre, width)
         grad_pre = grad_pre.astype(BF16)
         for tap in range(3):
-            window = x3[pl.ds(base + tap * width, size), :]
-            acc[tap * block : (tap + 1) * block, :] += mm(window.T, grad_pre)
+            window_t = x_last[tap] if last else x3[pl.ds(base + tap * width, size), :].T
+            acc[tap * block : (tap + 1) * block, :] += mm(window_t, grad_pre)
             finish(1 + tap)
 
     def grad_input(index):
@@ -462,6 +467,10 @@
         own_term(index)
 
     each(0, CHUNKS - 1, fill_in)
+    act_last[...] = own_gradient(CHUNKS - 1)
+    for tap in range(3):
+        start = (CHUNKS - 1) * size + tap * width
+        x_last[tap] = x3[start : start + size, :].T
     receive(CHUNKS - 1)
 
     @pl.when(frame == 3)
@@ -484,7 +493,7 @@
         for part_of in range(SPLIT):
             to_core(which * SPLIT + part_of)
 
-    backward(CHUNKS - 1, all_to_core)
+    backward(CHUNKS - 1, all_to_core, last=True)
 
     later = []
     actions = (to_first, to_second, to_y, back_z, back_x, back_core)
@@ -595,6 +604,8 @@
             pltpu.VMEM((3, block, channels), BF16),
             pltpu.VMEM((3, channels, channels), BF16),
             pltpu.VMEM((size, channels), F32),
+            pltpu.VMEM((channels, size), BF16),
+            pltpu.VMEM((3, block, size), BF16),
             pltpu.VMEM((count, channels), F32),
             pltpu.VMEM((count, lanes), F32),
             pltpu.VMEM((count, lanes), F32),

time: 95.3 us -> 94.2 us (0.988)
  local copies, waits for them, and re-layouts: 0.99 us -> 0 us
    unnamed x2 -> x0, local copies, waits for them, and re-layouts: 0.99 us -> none
where the time goes in v5:
time: 94.2 us; the launch traced here: 94.1 us
  Pallas kernels  93.4 us (99%)
    pallas_call x1, Pallas kernels, local(): pl.pallas_call(functools.partial(block_kernel, width, members, scale), ou...  90.4 us
    pallas_call x1, Pallas kernels, local(): pl.pallas_call(finish_kernel, out_shape=(frame, frame, jax.ShapeDtypeStru...  3.02 us

profile of v5, /device:TPU:0, one launch (start us, length us, event | category | flops | bytes accessed | tf_op | source)
XLA Modules:
  0.0 94.1 jit_solution(6373613123956977681)
XLA Ops:
  0.6 90.4 %video_block.1 = (bf16[4096,256]{1,0:T(8,128)(2,1)S(1)}, bf16[4096,256]{1,0:T(8,128)(2,1)S(1)}, bf16[3072,256]{1,0:T(8,128)(2,1)S(1)}) custom-call(bf16[4096,256]{1,0:T(8,128)(2,1)} %bitcast.8, bf16[4096,256]{1,0:T(8,128)(2,1)} %bitcast.9, bf16[3,768,256]{2,1,0:T(8,128)(2,1)} %bitcast.12, bf16[3,256,256]{2,1,0:T(8,128)(2,1)} %tw_hbm.1), custom_call_target="tpu_custom_call" | custom-call | flops 19327352832 | bytes 16777216 | tf_op jit(solution)/shard_map/video_block/pallas_call | solution.py:592
  91.0 3.0 %finish.1 = (bf16[4096,256]{1,0:T(8,128)(2,1)}, bf16[4096,256]{1,0:T(8,128)(2,1)}, f32[2304,256]{1,0:T(8,128)}, f32[768,256]{1,0:T(8,128)}) custom-call(bf16[4096,256]{1,0:T(8,128)(2,1)S(1)} %get-tuple-element.11.out, bf16[4096,256]{1,0:T(8,128)(2,1)S(1)} %get-tuple-element.12.gin, bf16[3072,256]{1,0:T(8,128)(2,1)S(1)} %get-tuple-element.13.grads), custom_call_target="tpu_custom_call" | custom-call | tf_op jit(solution)/shard_map/finish/pallas_call | solution.py:631

commit v6 on v5

--- a/solution.py
+++ b/solution.py
@@ -18,9 +18,9 @@
 SPLIT = 1
 X_FIRST_AT = ((0.5, 0.6), (3.5, 2.1), (8.0, 2.1), (10.8, 2.1), (15.2, 2.1), (18.0, 2.1))
 Z_FIRST_AT = ((0.5, 0.6), (8.0, 0.6), (11.0, 0.6), (13.8, 0.6), (18.3, 2.1), (20.9, 2.1))
-HELD_AT = (19.3,)
+HELD_AT = (17.3,)
 GRAD_INPUT_AT = ((1, 3.0), (0, 3.1))
-RELAY_AT = (2.5, 13.5, 21.6)
+RELAY_AT = (2.5, 12.0, 21.6)
 NOW = 2
 LAST_AT = (5.0, 17.2, 19.6)
 OWN_AT = 3.2

time: 94.2 us -> 93.1 us (0.988)
  Pallas kernels: 93.4 us -> 92.3 us
    pallas_call x1, Pallas kernels: 90.4 us -> 89.2 us  [local(): pl.pallas_call(functools.partial(block_kernel, width, members, scale), ou...]
where the time goes in v6:
time: 93.1 us; the launch traced here: 92.9 us
  Pallas kernels  92.3 us (99%)
    pallas_call x1, Pallas kernels, local(): pl.pallas_call(functools.partial(block_kernel, width, members, scale), ou...  89.2 us
    pallas_call x1, Pallas kernels, local(): pl.pallas_call(finish_kernel, out_shape=(frame, frame, jax.ShapeDtypeStru...  3.02 us

profile of v6, /device:TPU:0, one launch (start us, length us, event | category | flops | bytes accessed | tf_op | source)
XLA Modules:
  0.0 92.9 jit_solution(7508759464853133263)
XLA Ops:
  0.6 89.2 %video_block.1 = (bf16[4096,256]{1,0:T(8,128)(2,1)S(1)}, bf16[4096,256]{1,0:T(8,128)(2,1)S(1)}, bf16[3072,256]{1,0:T(8,128)(2,1)S(1)}) custom-call(bf16[4096,256]{1,0:T(8,128)(2,1)} %bitcast.8, bf16[4096,256]{1,0:T(8,128)(2,1)} %bitcast.9, bf16[3,768,256]{2,1,0:T(8,128)(2,1)} %bitcast.12, bf16[3,256,256]{2,1,0:T(8,128)(2,1)} %tw_hbm.1), custom_call_target="tpu_custom_call" | custom-call | flops 19327352832 | bytes 16777216 | tf_op jit(solution)/shard_map/video_block/pallas_call | solution.py:592
  89.9 3.0 %finish.1 = (bf16[4096,256]{1,0:T(8,128)(2,1)}, bf16[4096,256]{1,0:T(8,128)(2,1)}, f32[2304,256]{1,0:T(8,128)}, f32[768,256]{1,0:T(8,128)}) custom-call(bf16[4096,256]{1,0:T(8,128)(2,1)S(1)} %get-tuple-element.11.out, bf16[4096,256]{1,0:T(8,128)(2,1)S(1)} %get-tuple-element.12.gin, bf16[3072,256]{1,0:T(8,128)(2,1)S(1)} %get-tuple-element.13.grads), custom_call_target="tpu_custom_call" | custom-call | tf_op jit(solution)/shard_map/finish/pallas_call | solution.py:631
